TPU v7x, 256 devices: a whole 4x4x8 slice. The times are simulated.
256 devices in a mesh: section: 8 (over x, y_hi), member: 32 (over z, y_lo, core).
Axes of the slice: x: 4, y: 4 (y_hi: 2, y_lo: 2; y = y_hi * 2 + y_lo), z: 8, core: 2. Of those that a mesh axis runs over, the one named last changes fastest.
Arguments:
- populations: float32 [512, 19, 4096], P(('section', 'member'))
- fluid_mask: int32 [512, 4096], P(('section', 'member')), may hold values 0 or 1
- section_level: int32 [8], replicated, may hold values from 0 to 2, as said below
- neighbours: int32 [512, 18], P(('section', 'member')), may hold values from -1 to 511, as said below
- interface: int32 [512, 6, 4], P(('section', 'member')), may hold values from -1 to 511, as said below
Outputs:
- final_populations: float32 [512, 19, 4096], P(('section', 'member'))
Inputs may be any that keep to these rules, and one draw needn't show every extreme that they name: `section_level`: levels never fall along the section axis and each of 0, 1, 2 is held by some section. `neighbours`: A neighbour lies in the same section as the block, on the same member index or one beside it. `interface`: entries stand only on faces whose neighbour is -1; the named blocks lie in a section whose level differs from the block's by one, on the same member index or one beside it. Where that level is below the block's, exactly one quadrant of the face is named, else all four.
All inputs are finite; a program needn't handle non-finite values. No bound on the sum of `fluid_mask` on one device may be relied on, other than what follows from the above.
Results may differ from a plain program's by a relative error of at most 0.0003.
Values sent between devices are 32-bit elements; how exact they have to be, the bound alone decides.
A program may use at most 64 MiB of HBM per device.

v0:
```python
import jax
import jax.numpy as jnp
from jax import lax
from jax.experimental import pallas as pl
from jax.experimental.pallas import tpu as pltpu
from jax.sharding import PartitionSpec as P

MESH = pl.DeviceIdType.MESH
F32 = jnp.float32
NSEC = 8
NMEM = 32

VELOCITIES = (
    (0, 0, 0),
    (1, 0, 0),
    (-1, 0, 0),
    (0, 1, 0),
    (0, -1, 0),
    (0, 0, 1),
    (0, 0, -1),
    (1, 1, 0),
    (-1, -1, 0),
    (1, -1, 0),
    (-1, 1, 0),
    (1, 0, 1),
    (-1, 0, -1),
    (1, 0, -1),
    (-1, 0, 1),
    (0, 1, 1),
    (0, -1, -1),
    (0, 1, -1),
    (0, -1, 1),
)
OPPOSITE = (0, 2, 1, 4, 3, 6, 5, 8, 7, 10, 9, 12, 11, 14, 13, 16, 15, 18, 17)
SIDE_LISTS = tuple(
    tuple(tuple(q for q in range(19) if VELOCITIES[q][axis] == sign) for sign in (1, -1))
    for axis in range(3)
)


def side_of(q, axis):
    side = 0 if VELOCITIES[q][axis] > 0 else 1
    return side, SIDE_LISTS[axis][side].index(q)


def iotas(shape=(8, 128)):
    return lax.broadcasted_iota(jnp.int32, shape, 0), lax.broadcasted_iota(jnp.int32, shape, 1)


def lanes_from(x, index):
    return jnp.take_along_axis(x, index, axis=1)


def rows_from(x, index):
    return jnp.take_along_axis(x, index, axis=0)


def pick(cond, a, b):
    return lax.select(cond, a, b)


def tile_slices(axis, tile):
    first, second = 8 * (tile // 2), 128 * (tile % 2)
    return slice(first, first + 8), slice(second, second + 128)


def collide(cur, mask_ref, star, b, rate, advances):
    for tile in range(4):
        rows, lanes = tile_slices(0, tile)
        f = [cur[b, q, rows, lanes] for q in range(19)]
        density = f[0]
        for q in range(1, 19):
            density = density + f[q]
        velocity = []
        for axis in range(3):
            plus, minus = SIDE_LISTS[axis]
            momentum = f[plus[0]] - f[minus[0]]
            for i in range(1, 5):
                momentum = momentum + f[plus[i]]
            for i in range(1, 5):
                momentum = momentum - f[minus[i]]
            velocity.append(momentum / density)
        base = 1.0 - 1.5 * (
            velocity[0] * velocity[0] + velocity[1] * velocity[1] + velocity[2] * velocity[2]
        )
        fluid = mask_ref[b, rows, lanes] == 1
        keep = 1.0 - rate
        scaled = rate * density

        def put(q, relaxed):
            star[b, q, rows, lanes] = pick(
                advances, jnp.where(fluid, relaxed, f[OPPOSITE[q]]), f[q]
            )

        put(0, keep * f[0] + scaled * (1.0 / 3.0) * base)
        axis_weight = scaled * (1.0 / 18.0)
        edge_weight = scaled * (1.0 / 36.0)
        for q in range(1, 19, 2):
            c = VELOCITIES[q]
            along = None
            for axis in range(3):
                if c[axis]:
                    term = velocity[axis] if c[axis] > 0 else -velocity[axis]
                    along = term if along is None else along + term
            weight = axis_weight if q < 7 else edge_weight
            even = weight * (base + 4.5 * along * along)
            odd = weight * (3.0 * along)
            put(q, keep * f[q] + (even + odd))
            put(q + 1, keep * f[q + 1] + (even - odd))


def export(star, faces, b):
    row, lane = iotas()
    group, within = lane // 16, lane % 16
    for side in range(2):
        for p, q in enumerate(SIDE_LISTS[0][side]):
            layer = 15 if side == 0 else 0
            for half in range(2):
                faces[2 + b, 0, side * 2 + half, p : p + 1, :] = star[
                    b, q, layer : layer + 1, 128 * half : 128 * half + 128
                ]
    zero = jnp.zeros((8, 128), F32)
    for a in range(2):
        for side in range(2):
            total = zero
            for p, q in enumerate(SIDE_LISTS[1][side]):
                half = 1 - side
                x = star[b, q, 8 * a : 8 * a + 8, 128 * half : 128 * half + 128]
                shift = (16 * p + 16 if side == 0 else 16 * p) % 128
                x = pltpu.roll(x, shift, 1) if shift else x
                total = jnp.where(group == p, x, total)
            faces[2 + b, 1, a * 2 + side] = total
        for half in range(2):
            total = zero
            for side in range(2):
                for p, q in enumerate(SIDE_LISTS[2][side]):
                    x = star[b, q, 8 * a : 8 * a + 8, 128 * half : 128 * half + 128]
                    shift = 113 + p if side == 0 else 8 + p
                    x = pltpu.roll(x, shift, 1)
                    total = jnp.where(within == side * 8 + p, x, total)
            faces[2 + b, 2, a * 2 + half] = total


def restrict(faces, down, b):
    row, lane = iotas()
    group, within, low = lane // 16, lane % 16, lane % 8
    second = (lane // 8) % 2
    fine = group * 16 + 2 * low
    coarse = (2 * (group % 4)) * 16
    pair_rows = 2 * (row % 4)
    parts = []
    for side in range(2):
        halves = []
        for half in range(2):
            t = faces[2 + b, 0, side * 2 + half]
            t = t + pltpu.roll(t, 127, 1)
            t = t + pltpu.roll(t, 112, 1)
            halves.append(lanes_from(t, coarse + 2 * low))
        parts.append(jnp.where(group < 4, halves[0], halves[1]))
    down[3 * b] = 0.25 * jnp.where(second == 0, parts[0], parts[1])
    parts = []
    for side in range(2):
        rows = []
        for a in range(2):
            t = faces[2 + b, 1, a * 2 + side]
            t = t + pltpu.roll(t, 127, 1)
            t = t + pltpu.roll(t, 7, 0)
            rows.append(rows_from(lanes_from(t, fine), pair_rows))
        parts.append(jnp.where(row < 4, rows[0], rows[1]))
    down[3 * b + 1] = 0.25 * jnp.where(second == 0, parts[0], parts[1])
    rows = []
    for a in range(2):
        halves = []
        for half in range(2):
            t = faces[2 + b, 2, a * 2 + half]
            t = t + pltpu.roll(t, 112, 1)
            halves.append(lanes_from(t, coarse + within))
        t = jnp.where(group < 4, halves[0], halves[1])
        t = t + pltpu.roll(t, 7, 0)
        rows.append(rows_from(t, pair_rows))
    down[3 * b + 2] = 0.25 * jnp.where(row < 4, rows[0], rows[1])


def slot_of(block, member):
    safe = jnp.maximum(block, 0)
    offset = lax.rem(lax.div(safe, 2), NMEM) - member + 1
    return jnp.clip(offset * 2 + lax.rem(safe, 2), 0, 5)


def select_quadrants(faces, wanted, out, other, member):
    row, lane = iotas()
    second = (lane // 8) % 2
    for b in range(2):
        for axis in range(3):
            parts = []
            for side in range(2):
                code = jnp.maximum(wanted[other, b * 6 + 2 * axis + 1 - side], 0)
                quadrant = lax.rem(code, 4)
                first, last = lax.div(quadrant, 2), lax.rem(quadrant, 2)
                slot = slot_of(lax.div(code, 4), member)
                if axis == 0:
                    tile = side * 2 + first
                elif axis == 1:
                    tile = first * 2 + side
                else:
                    tile = quadrant
                t = faces[slot, axis, tile]
                if axis < 2:
                    t = pick(last == side, t, pltpu.roll(t, 8 if side else 120, 1))
                parts.append(t)
            out[other, b * 3 + axis] = jnp.where(second == 0, parts[0], parts[1])


def build_halo(faces, up, down, halo, b, nbr, link, wanted, level, own, member):
    row, lane = iotas()
    group, within, low = lane // 16, lane % 16, lane % 8
    second = (lane // 8) % 2
    spread_rows = [4 * a + row // 2 for a in range(2)]

    def link_state(j):
        code = wanted[b * 6 + j]
        section = lax.div(lax.div(jnp.maximum(code, 0), 4), 2 * NMEM)
        any_link = code >= 0
        coarse = level[section] < own
        return section, any_link, coarse

    def means(axis, j, k):
        block = link[(b * 6 + j) * 4 + k]
        safe = jnp.maximum(block, 0)
        section = lax.div(safe, 2 * NMEM)
        offset = jnp.clip(lax.rem(lax.div(safe, 2), NMEM) - member + 1, 0, 2)
        t = down[section, offset, lax.rem(safe, 2) * 3 + axis]
        return pick(block >= 0, t, jnp.zeros_like(t))

    for axis in range(3):
        states, near, quads, ups = [], [], [], []
        for side in range(2):
            j = 2 * axis + 1 - side
            section, any_link, coarse = link_state(j)
            states.append((nbr[b * 18 + j] >= 0, any_link, coarse))
            near.append(slot_of(nbr[b * 18 + j], member))
            ups.append(up[section, b * 3 + axis])
            if down is not None:
                quads.append([means(axis, j, k) for k in range(4)])
        if axis == 0:
            rest = jnp.where(row == 0, F32(1.0 / 18.0), F32(1.0 / 36.0))
        elif axis == 1:
            rest = jnp.where(group == 0, F32(1.0 / 18.0), F32(1.0 / 36.0))
        else:
            rest = jnp.where(low == 0, F32(1.0 / 18.0), F32(1.0 / 36.0))

        def choose(side, tile, from_up, from_down):
            is_near, any_link, coarse = states[side]
            linked = from_up if from_down is None else pick(coarse, from_up, from_down)
            far = pick(any_link, linked, rest)
            return pick(is_near, faces[near[side], axis, tile], far)

        if axis < 2:
            for side in range(2):
                if axis == 1:
                    wide = lanes_from(ups[side], group * 16 + side * 8 + within // 2)
                for a in range(2):
                    if axis == 0:
                        tile = side * 2 + a
                        from_up = lanes_from(
                            ups[side], (4 * a + group // 2) * 16 + side * 8 + within // 2
                        )
                    else:
                        tile = a * 2 + side
                        from_up = rows_from(wide, spread_rows[a])
                    from_down = None
                    if down is not None:
                        low_part, high_part = quads[side][2 * a], quads[side][2 * a + 1]
                        if side:
                            low_part = pltpu.roll(low_part, 120, 1)
                        else:
                            high_part = pltpu.roll(high_part, 8, 1)
                        from_down = jnp.where(second == 0, low_part, high_part)
                    rows, lanes = tile_slices(axis, tile)
                    halo[axis, rows, lanes] = choose(side, tile, from_up, from_down)
        else:
            both = jnp.where(second == 0, ups[0], ups[1])
            for half in range(2):
                wide = lanes_from(both, (4 * half + group // 2) * 16 + within)
                for a in range(2):
                    tile = a * 2 + half
                    from_up = rows_from(wide, spread_rows[a])
                    parts = [
                        choose(side, tile, from_up, quads[side][tile] if down is not None else None)
                        for side in range(2)
                    ]
                    rows, lanes = tile_slices(axis, tile)
                    halo[axis, rows, lanes] = jnp.where(second == 0, parts[0], parts[1])

    for q in range(7, 19):
        c = VELOCITIES[q]
        one, two = [axis for axis in range(3) if c[axis]]
        side, p = side_of(q, two)
        block = nbr[b * 18 + OPPOSITE[q] - 1]
        slot = slot_of(block, member)
        far_end = c[one] > 0
        if two == 1:
            tiles = [(1 if far_end else 0) * 2 + side]
            where = (row == (7 if far_end else 0)) & (group == p)
        elif one == 0:
            tiles = [(1 if far_end else 0) * 2 + half for half in range(2)]
            where = (row == (7 if far_end else 0)) & (within == side * 8 + p)
        else:
            tiles = [a * 2 + (1 if far_end else 0) for a in range(2)]
            where = lane == (7 if far_end else 0) * 16 + side * 8 + p
        for tile in tiles:
            rows, lanes = tile_slices(two, tile)
            line = faces[slot, two, tile]
            line = pick(block >= 0, line, jnp.full_like(line, 1.0 / 36.0))
            halo[two, rows, lanes] = jnp.where(where, line, halo[two, rows, lanes])


def stream(star, halo, out, b, advances):
    row, lane = iotas((16, 128))
    within = lane % 16
    first, last = lane < 16, lane >= 112

    def roll(x, shift, axis):
        shift %= x.shape[axis]
        return pltpu.roll(x, shift, axis) if shift else x

    def ring(left, right, sign):
        a, c = roll(left, 16 * sign, 1), roll(right, 16 * sign, 1)
        if sign > 0:
            return jnp.where(first, c, a), jnp.where(first, a, c)
        return jnp.where(last, c, a), jnp.where(last, a, c)

    for q in range(19):
        c = VELOCITIES[q]
        old = [star[b, q, :, 128 * half : 128 * half + 128] for half in range(2)]
        new = list(old)
        if c[0]:
            side, p = side_of(q, 0)
            place = side * 8 + p
            for half in range(2):
                plane = halo[0, place : place + 1, 128 * half : 128 * half + 128]
                moved = roll(new[half], c[0], 0)
                new[half] = jnp.where(row == (0 if c[0] > 0 else 15), plane, moved)
        if c[1]:
            side, p = side_of(q, 1)
            border = halo[1, :, 128 * side : 128 * side + 128]
            border = roll(border, -16 * p if side == 0 else 112 - 16 * p, 1)
            if c[0]:
                border = roll(border, c[0], 0)
            a, d = roll(new[0], 16 * c[1], 1), roll(new[1], 16 * c[1], 1)
            if c[1] > 0:
                new = [jnp.where(first, border, a), jnp.where(first, a, d)]
            else:
                new = [jnp.where(last, d, a), jnp.where(last, border, d)]
        if c[2]:
            side, p = side_of(q, 2)
            borders = []
            for half in range(2):
                border = halo[2, :, 128 * half : 128 * half + 128]
                border = roll(border, -p if side == 0 else 7 - p, 1)
                if c[0]:
                    border = roll(border, c[0], 0)
                borders.append(border)
            if c[1]:
                borders = ring(borders[0], borders[1], c[1])
            for half in range(2):
                new[half] = jnp.where(
                    within == (0 if c[2] > 0 else 15), borders[half], roll(new[half], c[2], 1)
                )
        for half in range(2):
            out[b, q, :, 128 * half : 128 * half + 128] = pick(advances, new[half], old[half])


def kernel(
    pop,
    mask_ref,
    level,
    nbr,
    link,
    out,
    star,
    middle,
    faces_a,
    faces_b,
    up_send_a,
    up_send_b,
    up_a,
    up_b,
    down_send,
    down,
    halo,
    wanted_own,
    wanted,
    meta_ss,
    meta_rs,
    mem_ss,
    mem_rs,
    up_ss,
    up_rs,
    down_ss,
    down_rs,
):
    s = lax.axis_index("section")
    m = lax.axis_index("member")
    own = level[s]
    rate = jnp.where(
        own == 0, F32(1.0 / 0.55), jnp.where(own == 1, F32(1.0 / 0.6), F32(1.0 / 0.7))
    )
    has = {-1: m > 0, 0: None, 1: m < NMEM - 1}

    def if_member(dm, do):
        if has[dm] is None:
            do()
        else:
            pl.when(has[dm])(do)

    barrier = pltpu.get_barrier_semaphore()

    def greet(other, dm):
        pl.semaphore_signal(barrier, inc=1, device_id=(other, m + dm), device_id_type=MESH)

    def greet_section(other, carry):
        @pl.when(other != s)
        def _():
            greet(other, 0)

        for dm in (-1, 1):
            if_member(dm, lambda dm=dm: greet(other, dm))
        return carry

    lax.fori_loop(0, NSEC, greet_section, 0)
    for i in range(12):
        code = jnp.int32(-1)
        for k in range(4):
            block = link[i * 4 + k]
            code = jnp.maximum(code, jnp.where(block >= 0, block * 4 + k, -1))
        wanted_own[i] = code

    def first_part(b, carry):
        collide(pop, mask_ref, star, b, rate, own >= 1)
        export(star, faces_a, b)
        restrict(faces_a, down_send, b)
        return carry

    lax.fori_loop(0, 2, first_part, 0)

    one = jnp.int32(1)
    there = jnp.where(m > 0, one, 0) + jnp.where(m < NMEM - 1, one, 0)
    pl.semaphore_wait(barrier, NSEC * (there + 1) - 1)

    def meta_copy(place, other):
        return pltpu.make_async_remote_copy(
            src_ref=wanted_own,
            dst_ref=wanted.at[place],
            send_sem=meta_ss.at[other],
            recv_sem=meta_rs.at[place],
            device_id=(other, m),
            device_id_type=MESH,
        )

    def mem_copy(faces, step, dm, arriving):
        into = (2 + 2 * dm) if arriving else (2 - 2 * dm)
        return pltpu.make_async_remote_copy(
            src_ref=faces.at[pl.ds(2, 2)],
            dst_ref=faces.at[pl.ds(into, 2)],
            send_sem=mem_ss.at[step, (dm + 1) // 2],
            recv_sem=mem_rs.at[step, into // 4],
            device_id=(s, m + dm),
            device_id_type=MESH,
        )

    def up_copy(sends, receives, step, other, place):
        return pltpu.make_async_remote_copy(
            src_ref=sends.at[other],
            dst_ref=receives.at[place],
            send_sem=up_ss.at[step, other],
            recv_sem=up_rs.at[step, place],
            device_id=(other, m),
            device_id_type=MESH,
        )

    def down_copy(other, dm, place, offset):
        return pltpu.make_async_remote_copy(
            src_ref=down_send,
            dst_ref=down.at[place, offset],
            send_sem=down_ss.at[other, dm + 1],
            recv_sem=down_rs.at[place, offset],
            device_id=(other, m + dm),
            device_id_type=MESH,
        )

    def each(low, high, do):
        def step(i, carry):
            do(i)
            return carry

        lax.fori_loop(low, high, step, 0)

    each(0, s, lambda other: meta_copy(s, other).start())
    for dm in (-1, 1):
        if_member(dm, lambda dm=dm: mem_copy(faces_a, 0, dm, False).start())

    def start_down(other):
        for dm in (-1, 0, 1):
            if_member(dm, lambda dm=dm: down_copy(other, dm, s, 1 - dm).start())

    each(1, s, start_down)

    def exchange(faces, sends, receives, step, low, high):
        for dm in (-1, 1):
            if_member(dm, lambda dm=dm: mem_copy(faces, step, dm, True).wait_recv())
        if step == 0:
            each(s + 1, NSEC, lambda other: meta_copy(other, s).wait_recv())

        def send(other):
            select_quadrants(faces, wanted, sends, other, m)
            up_copy(sends, receives, step, other, s).start()

        each(high, NSEC, send)
        each(low, s, lambda other: up_copy(sends, receives, step, s, other).wait_recv())

    exchange(faces_a, up_send_a, up_a, 0, 0, s + 1)

    def wait_down(other):
        for dm in (-1, 0, 1):
            if_member(dm, lambda dm=dm: down_copy(s, dm, other, dm + 1).wait_recv())

    each(jnp.where(s == 0, NSEC, s + 1), NSEC, wait_down)

    def second_part(b, carry):
        build_halo(faces_a, up_a, down, halo, b, nbr, link, wanted_own, level, own, m)
        stream(star, halo, middle, b, own >= 1)
        return carry

    lax.fori_loop(0, 2, second_part, 0)

    def third_part(b, carry):
        collide(middle, mask_ref, star, b, rate, own == 2)
        export(star, faces_b, b)
        return carry

    lax.fori_loop(0, 2, third_part, 0)
    for dm in (-1, 1):
        if_member(dm, lambda dm=dm: mem_copy(faces_b, 1, dm, False).start())
    exchange(faces_b, up_send_b, up_b, 1, 1, jnp.where(s == 0, NSEC, s + 1))

    def fourth_part(b, carry):
        build_halo(faces_b, up_b, None, halo, b, nbr, link, wanted_own, level, own, m)
        stream(star, halo, out, b, own == 2)
        return carry

    lax.fori_loop(0, 2, fourth_part, 0)

    each(0, s, lambda other: meta_copy(s, other).wait_send())
    for dm in (-1, 1):
        if_member(dm, lambda dm=dm: mem_copy(faces_a, 0, dm, False).wait_send())
        if_member(dm, lambda dm=dm: mem_copy(faces_b, 1, dm, False).wait_send())

    def end_down(other):
        for dm in (-1, 0, 1):
            if_member(dm, lambda dm=dm: down_copy(other, dm, s, 1 - dm).wait_send())

    each(1, s, end_down)
    each(s + 1, NSEC, lambda other: up_copy(up_send_a, up_a, 0, other, s).wait_send())
    each(
        jnp.where(s == 0, NSEC, s + 1),
        NSEC,
        lambda other: up_copy(up_send_b, up_b, 1, other, s).wait_send(),
    )


def body(populations, fluid_mask, section_level, neighbours, interface):
    state = pltpu.VMEM((2, 19, 16, 256), F32)
    faces = pltpu.VMEM((6, 3, 4, 8, 128), F32)
    ups = pltpu.VMEM((NSEC, 6, 8, 128), F32)
    vmem = pl.BlockSpec(memory_space=pltpu.VMEM)
    smem = pl.BlockSpec(memory_space=pltpu.SMEM)
    dma = pltpu.SemaphoreType.DMA
    out = pl.pallas_call(
        kernel,
        out_shape=jax.ShapeDtypeStruct((2, 19, 16, 256), F32),
        in_specs=[vmem, vmem, smem, smem, smem],
        out_specs=vmem,
        scratch_shapes=[
            state,
            state,
            faces,
            faces,
            ups,
            ups,
            ups,
            ups,
            pltpu.VMEM((6, 8, 128), F32),
            pltpu.VMEM((NSEC, 3, 6, 8, 128), F32),
            pltpu.VMEM((3, 16, 256), F32),
            pltpu.SMEM((12,), jnp.int32),
            pltpu.SMEM((NSEC, 12), jnp.int32),
            dma((NSEC,)),
            dma((NSEC,)),
            dma((2, 2)),
            dma((2, 2)),
            dma((2, NSEC)),
            dma((2, NSEC)),
            dma((NSEC, 3)),
            dma((NSEC, 3)),
        ],
        compiler_params=pltpu.CompilerParams(
            collective_id=0, has_side_effects=True, vmem_limit_bytes=32 * 1024 * 1024
        ),
        name="lattice_step",
    )(
        populations.reshape(2, 19, 16, 256),
        fluid_mask.reshape(2, 16, 256),
        section_level,
        neighbours.reshape(36),
        interface.reshape(48),
    )
    return out.reshape(2, 19, 4096)


def solution(mesh):
    return jax.shard_map(
        body,
        mesh=mesh,
        in_specs=(
            P(("section", "member"), None, None),
            P(("section", "member"), None),
            P(),
            P(("section", "member"), None),
            P(("section", "member"), None, None),
        ),
        out_specs=P(("section", "member"), None, None),
        check_vma=False,
    )
```

profile of v0, /device:TPU:135, one launch (start us, length us, event | category | flops | bytes accessed | tf_op | source)
XLA Modules:
  0.0 35.7 jit_solution(14076192669776187732)
XLA Ops:
  0.0 0.0 copy-start.1
  0.0 0.7 %copy-done.1 = s32[2,18]{1,0:T(2,128)S(1)} copy-done((s32[2,18]{1,0:T(2,128)S(1)}, s32[2,18]{1,0:T(2,128)}, u32[]{:S(2)}) %copy-start.1) | copy-done | bytes 168
  0.7 0.1 reshape.17.nbr
  0.8 0.8 %copy.9 = s32[2,6,4]{2,1,0:T(8,128)S(1)} copy(s32[2,6,4]{1,2,0:T(4,128)} %param.9) | data formatting | bytes 384 | tf_op args[4]
  1.5 0.1 reshape.18.link
  1.6 0.8 %copy.14 = s32[1,2,16,256]{3,2,1,0:T(8,128)S(1)} copy(s32[1,2,16,256]{3,1,2,0:T(2,128)} %bitcast.11) | data formatting | bytes 65536
  2.4 1.6 %reshape.15 = f32[2,19,16,256]{3,2,0,1:T(8,128)S(1)} reshape(f32[2,19,4096]{2,0,1:T(2,128)} %param.5) | data formatting | bytes 1245184 | tf_op jit(solution)/shard_map/reshape | solution.py:612
  4.0 0.0 copy-start
  4.1 0.6 %copy-done = s32[8]{0:T(128)S(1)} copy-done((s32[8]{0:T(128)S(1)}, s32[8]{0:T(128)}, u32[]{:S(2)}) %copy-start) | copy-done | bytes 56
  4.7 29.8 %lattice_step.1 = f32[2,19,16,256]{3,2,1,0:T(8,128)S(1)} custom-call(f32[2,19,16,256]{3,2,1,0:T(8,128)S(1)} %copy.10.pop, s32[2,16,256]{2,1,0:T(8,128)S(1)} %bitcast.10, s32[8]{0:T(128)S(1)} %copy-done, s32[36]{0:T(128)S(1)} %reshape.17.nbr, s32[48]{0:T(128)S(1)} %reshape.18.link), custom_call_target="tpu_custom_call" | custom-call | tf_op jit(solution)/shard_map/lattice_step/pallas_call | solution.py:579
  34.5 1.2 %reshape.19 = f32[2,19,4096]{2,0,1:T(2,128)} reshape(f32[2,19,16,256]{3,2,0,1:T(8,128)S(1)} %copy.11) | data formatting | bytes 1245184 | tf_op jit(solution)/shard_map/reshape | solution.py:618
  (2 shorter events, 0.1 us)
Async XLA Ops:
  0.0 0.7 %copy-start.1 = (s32[2,18]{1,0:T(2,128)S(1)}, s32[2,18]{1,0:T(2,128)}, u32[]{:S(2)}) copy-start(s32[2,18]{1,0:T(2,128)} %param.8) | copy-start | bytes 436
  4.0 0.7 %copy-start = (s32[8]{0:T(128)S(1)}, s32[8]{0:T(128)}, u32[]{:S(2)}) copy-start(s32[8]{0:T(128)} %level.1) | copy-start | bytes 100
where the time goes:
time: 36.1 us; the launch traced here: 35.7 us
  Pallas kernels  29.8 us (83%)
  local copies, waits for them, and re-layouts  5.91 us (16%)
    pallas_call x1, Pallas kernels, body(): pl.pallas_call(kernel, out_shape=jax.ShapeDtypeStruct((2, 19, 16, 256), F...  29.8 us
    unnamed x6, local copies, waits for them, and re-layouts  2.82 us
    reshape x2, local copies, waits for them, and re-layouts, body(): populations.reshape(2, 19, 16, 256)  1.65 us
    reshape x1, local copies, waits for them, and re-layouts, body(): return out.reshape(2, 19, 4096)  1.23 us

commit v1 on v0

--- a/solution.py
+++ b/solution.py
@@ -64,10 +64,17 @@
     return slice(first, first + 8), slice(second, second + 128)
 
 
-def collide(cur, mask_ref, star, b, rate, advances):
+def woven(b, tile):
+    return pl.ds(32 * (tile // 2) + 2 * (tile % 2) + b, 8, stride=4)
+
+
+def collide(cur, mask_ref, star, b, rate, advances, first):
     for tile in range(4):
         rows, lanes = tile_slices(0, tile)
-        f = [cur[b, q, rows, lanes] for q in range(19)]
+        if first:
+            f = [cur[q, woven(b, tile), :] for q in range(19)]
+        else:
+            f = [cur[b, q, rows, lanes] for q in range(19)]
         density = f[0]
         for q in range(1, 19):
             density = density + f[q]
@@ -83,7 +90,7 @@
         base = 1.0 - 1.5 * (
             velocity[0] * velocity[0] + velocity[1] * velocity[1] + velocity[2] * velocity[2]
         )
-        fluid = mask_ref[b, rows, lanes] == 1
+        fluid = mask_ref[woven(b, tile), :] == 1
         keep = 1.0 - rate
         scaled = rate * density
 
@@ -225,7 +232,7 @@
         return section, any_link, coarse
 
     def means(axis, j, k):
-        block = link[(b * 6 + j) * 4 + k]
+        block = link[b, k, j]
         safe = jnp.maximum(block, 0)
         section = lax.div(safe, 2 * NMEM)
         offset = jnp.clip(lax.rem(lax.div(safe, 2), NMEM) - member + 1, 0, 2)
@@ -237,8 +244,8 @@
         for side in range(2):
             j = 2 * axis + 1 - side
             section, any_link, coarse = link_state(j)
-            states.append((nbr[b * 18 + j] >= 0, any_link, coarse))
-            near.append(slot_of(nbr[b * 18 + j], member))
+            states.append((nbr[b, j] >= 0, any_link, coarse))
+            near.append(slot_of(nbr[b, j], member))
             ups.append(up[section, b * 3 + axis])
             if down is not None:
                 quads.append([means(axis, j, k) for k in range(4)])
@@ -296,7 +303,7 @@
         c = VELOCITIES[q]
         one, two = [axis for axis in range(3) if c[axis]]
         side, p = side_of(q, two)
-        block = nbr[b * 18 + OPPOSITE[q] - 1]
+        block = nbr[b, OPPOSITE[q] - 1]
         slot = slot_of(block, member)
         far_end = c[one] > 0
         if two == 1:
@@ -315,7 +322,7 @@
             halo[two, rows, lanes] = jnp.where(where, line, halo[two, rows, lanes])
 
 
-def stream(star, halo, out, b, advances):
+def stream(star, halo, out, b, advances, final):
     row, lane = iotas((16, 128))
     within = lane % 16
     first, last = lane < 16, lane >= 112
@@ -368,16 +375,27 @@
                     within == (0 if c[2] > 0 else 15), borders[half], roll(new[half], c[2], 1)
                 )
         for half in range(2):
-            out[b, q, :, 128 * half : 128 * half + 128] = pick(advances, new[half], old[half])
+            result = pick(advances, new[half], old[half])
+            if final:
+                for a in range(2):
+                    out[q, woven(b, 2 * a + half), :] = result[8 * a : 8 * a + 8]
+            else:
+                out[b, q, :, 128 * half : 128 * half + 128] = result
 
 
 def kernel(
+    pop_hbm,
+    mask_hbm,
+    level_hbm,
+    nbr_hbm,
+    link_hbm,
+    out,
     pop,
     mask_ref,
     level,
     nbr,
     link,
-    out,
+    in_sems,
     star,
     middle,
     faces_a,
@@ -402,10 +420,20 @@
 ):
     s = lax.axis_index("section")
     m = lax.axis_index("member")
-    own = level[s]
-    rate = jnp.where(
-        own == 0, F32(1.0 / 0.55), jnp.where(own == 1, F32(1.0 / 0.6), F32(1.0 / 0.7))
-    )
+    loads = [
+        pltpu.make_async_copy(src, dst, in_sems.at[i])
+        for i, (src, dst) in enumerate(
+            [
+                (level_hbm, level),
+                (link_hbm, link),
+                (nbr_hbm, nbr),
+                (pop_hbm, pop),
+                (mask_hbm, mask_ref),
+            ]
+        )
+    ]
+    for load in loads:
+        load.start()
     has = {-1: m > 0, 0: None, 1: m < NMEM - 1}
 
     def if_member(dm, do):
@@ -429,15 +457,21 @@
         return carry
 
     lax.fori_loop(0, NSEC, greet_section, 0)
+    for load in loads:
+        load.wait()
+    own = level[s]
+    rate = jnp.where(
+        own == 0, F32(1.0 / 0.55), jnp.where(own == 1, F32(1.0 / 0.6), F32(1.0 / 0.7))
+    )
     for i in range(12):
         code = jnp.int32(-1)
         for k in range(4):
-            block = link[i * 4 + k]
+            block = link[i // 6, k, i % 6]
             code = jnp.maximum(code, jnp.where(block >= 0, block * 4 + k, -1))
         wanted_own[i] = code
 
     def first_part(b, carry):
-        collide(pop, mask_ref, star, b, rate, own >= 1)
+        collide(pop, mask_ref, star, b, rate, own >= 1, True)
         export(star, faces_a, b)
         restrict(faces_a, down_send, b)
         return carry
@@ -529,13 +563,13 @@
 
     def second_part(b, carry):
         build_halo(faces_a, up_a, down, halo, b, nbr, link, wanted_own, level, own, m)
-        stream(star, halo, middle, b, own >= 1)
+        stream(star, halo, middle, b, own >= 1, False)
         return carry
 
     lax.fori_loop(0, 2, second_part, 0)
 
     def third_part(b, carry):
-        collide(middle, mask_ref, star, b, rate, own == 2)
+        collide(middle, mask_ref, star, b, rate, own == 2, False)
         export(star, faces_b, b)
         return carry
 
@@ -546,7 +580,7 @@
 
     def fourth_part(b, carry):
         build_halo(faces_b, up_b, None, halo, b, nbr, link, wanted_own, level, own, m)
-        stream(star, halo, out, b, own == 2)
+        stream(star, halo, out, b, own == 2, True)
         return carry
 
     lax.fori_loop(0, 2, fourth_part, 0)
@@ -574,14 +608,20 @@
     faces = pltpu.VMEM((6, 3, 4, 8, 128), F32)
     ups = pltpu.VMEM((NSEC, 6, 8, 128), F32)
     vmem = pl.BlockSpec(memory_space=pltpu.VMEM)
-    smem = pl.BlockSpec(memory_space=pltpu.SMEM)
+    hbm = pl.BlockSpec(memory_space=pltpu.HBM)
     dma = pltpu.SemaphoreType.DMA
     out = pl.pallas_call(
         kernel,
-        out_shape=jax.ShapeDtypeStruct((2, 19, 16, 256), F32),
-        in_specs=[vmem, vmem, smem, smem, smem],
+        out_shape=jax.ShapeDtypeStruct((19, 64, 128), F32),
+        in_specs=[hbm] * 5,
         out_specs=vmem,
         scratch_shapes=[
+            pltpu.VMEM((19, 64, 128), F32),
+            pltpu.VMEM((64, 128), jnp.int32),
+            pltpu.SMEM((NSEC,), jnp.int32),
+            pltpu.SMEM((2, 18), jnp.int32),
+            pltpu.SMEM((2, 4, 6), jnp.int32),
+            dma((5,)),
             state,
             state,
             faces,
@@ -605,17 +645,17 @@
             dma((NSEC, 3)),
         ],
         compiler_params=pltpu.CompilerParams(
-            collective_id=0, has_side_effects=True, vmem_limit_bytes=32 * 1024 * 1024
+            collective_id=0, has_side_effects=True, vmem_limit_bytes=62 * 1024 * 1024
         ),
         name="lattice_step",
     )(
-        populations.reshape(2, 19, 16, 256),
-        fluid_mask.reshape(2, 16, 256),
+        populations.reshape(2, 19, 32, 128).transpose(1, 2, 0, 3).reshape(19, 64, 128),
+        fluid_mask.reshape(2, 32, 128).transpose(1, 0, 2).reshape(64, 128),
         section_level,
-        neighbours.reshape(36),
-        interface.reshape(48),
+        neighbours,
+        interface.transpose(0, 2, 1),
     )
-    return out.reshape(2, 19, 4096)
+    return out.reshape(19, 32, 2, 128).transpose(2, 0, 1, 3).reshape(2, 19, 4096)
 
 
 def solution(mesh):

time: 36.1 us -> 32.6 us (0.903)
  local copies, waits for them, and re-layouts: 5.91 us -> 1.96 us
    reshape x5 -> x0, local copies, waits for them, and re-layouts: 3.05 us -> none  [the longest x2 1.65 us: body(): populations.reshape(2, 19, 16, 256)]
    unnamed x6 -> x1, local copies, waits for them, and re-layouts: 2.82 us -> 1.96 us
where the time goes in v1:
time: 32.6 us; the launch traced here: 32 us
  Pallas kernels  30 us (92%)
  local copies, waits for them, and re-layouts  1.96 us (6%)
    pallas_call x1, Pallas kernels, body(): pl.pallas_call(kernel, out_shape=jax.ShapeDtypeStruct((19, 64, 128), F32)...  30 us
    unnamed x1, local copies, waits for them, and re-layouts  1.96 us

profile of v1, /device:TPU:135, one launch (start us, length us, event | category | flops | bytes accessed | tf_op | source)
XLA Modules:
  0.0 32.0 jit_solution(15375413899736156334)
XLA Ops:
  0.0 30.0 %lattice_step.1 = f32[19,64,128]{2,1,0:T(8,128)} custom-call(f32[19,64,128]{2,1,0:T(8,128)} %bitcast.17, s32[64,128]{1,0:T(8,128)} %bitcast.18, s32[8]{0:T(128)} %level_hbm.1, s32[2,18]{1,0:T(2,128)} %nbr_hbm.1, s32[2,4,6]{2,1,0:T(4,128)} %bitcast.19), custom_call_target="tpu_custom_call" | custom-call | tf_op jit(solution)/shard_map/lattice_step/pallas_call | solution.py:613
  30.0 2.0 %copy.10 = f32[2,19,4096]{2,0,1:T(2,128)} copy(f32[2,19,4096]{2,0,1:T(2,128)} %bitcast.16) | data formatting | bytes 1245184

commit v2 on v1

--- a/solution.py
+++ b/solution.py
@@ -64,6 +64,69 @@
     return slice(first, first + 8), slice(second, second + 128)
 
 
+def packing(count):
+    packed = -(-count * 5 // 8)
+    spare = [(d, g) for d in range(packed) for g in (5, 6, 7)]
+    runs = []
+    for source in range(packed, count):
+        for group in range(5):
+            d, g = spare.pop(0)
+            last = runs[-1] if runs else None
+            if last and last[0] == source and last[2] == d and last[3] + last[4] == g:
+                runs[-1] = last[:4] + (last[4] + 1,)
+            else:
+                runs.append((source, group, d, g, 1))
+    return packed, runs
+
+
+def lane_roll(x, shift):
+    shift %= 128
+    return pltpu.roll(x, shift, 1) if shift else x
+
+
+def pack(tiles):
+    lane = iotas()[1]
+    packed, runs = packing(len(tiles))
+    result = list(tiles[:packed])
+    for source, group, d, g, length in runs:
+        moved = lane_roll(tiles[source], 16 * (g - group))
+        inside = (lane >= 16 * g) & (lane < 16 * (g + length))
+        result[d] = jnp.where(inside, moved, result[d])
+    return result
+
+
+def unpack(load, source, count):
+    lane = iotas()[1]
+    packed, runs = packing(count)
+    if source < packed:
+        return load(source)
+    result = None
+    for which, group, d, g, length in runs:
+        if which == source:
+            moved = lane_roll(load(d), 16 * (group - g))
+            result = moved if result is None else jnp.where(lane >= 16 * group, moved, result)
+    return result
+
+
+def store_message(tiles, put):
+    for d, t in enumerate(pack([tiles[1], tiles[2], tiles[4], tiles[5]])):
+        put(8 * d, t)
+    for b in range(2):
+        put(24 + 5 * b, tiles[3 * b][0:5])
+
+
+def message_tile(load, axis, block):
+    if axis == 0:
+        pair = load(24), load(29)
+    else:
+        pair = tuple(unpack(lambda d: load(8 * d), 2 * b + axis - 1, 4) for b in range(2))
+    return pick(block == 0, pair[0], pair[1])
+
+
+def face_order(lane):
+    return (lane % 8) * 16 + lane // 8 % 2 * 8 + lane // 16
+
+
 def woven(b, tile):
     return pl.ds(32 * (tile // 2) + 2 * (tile % 2) + b, 8, stride=4)
 
@@ -116,17 +179,20 @@
             put(q + 1, keep * f[q + 1] + (even - odd))
 
 
-def export(star, faces, b):
+def export(star, faces, message, b):
     row, lane = iotas()
     group, within = lane // 16, lane % 16
     for side in range(2):
         for p, q in enumerate(SIDE_LISTS[0][side]):
             layer = 15 if side == 0 else 0
             for half in range(2):
-                faces[2 + b, 0, side * 2 + half, p : p + 1, :] = star[
-                    b, q, layer : layer + 1, 128 * half : 128 * half + 128
-                ]
+                line = star[b, q, layer : layer + 1, 128 * half : 128 * half + 128]
+                place = side * 2 + half
+                faces[2 + b, 0, place, p : p + 1, :] = line
+                message[b, 40 + 5 * place + p : 41 + 5 * place + p, :] = line
     zero = jnp.zeros((8, 128), F32)
+    tiles = [None] * 8
+    order = face_order(lane)
     for a in range(2):
         for side in range(2):
             total = zero
@@ -136,7 +202,7 @@
                 shift = (16 * p + 16 if side == 0 else 16 * p) % 128
                 x = pltpu.roll(x, shift, 1) if shift else x
                 total = jnp.where(group == p, x, total)
-            faces[2 + b, 1, a * 2 + side] = total
+            tiles[a * 2 + side] = total
         for half in range(2):
             total = zero
             for side in range(2):
@@ -145,10 +211,36 @@
                     shift = 113 + p if side == 0 else 8 + p
                     x = pltpu.roll(x, shift, 1)
                     total = jnp.where(within == side * 8 + p, x, total)
-            faces[2 + b, 2, a * 2 + half] = total
-
-
-def restrict(faces, down, b):
+            tiles[4 + a * 2 + half] = lanes_from(total, order)
+    for i, t in enumerate(tiles):
+        faces[2 + b, 1 + i // 4, i % 4] = t
+    for d, t in enumerate(pack(tiles)):
+        message[b, 8 * d : 8 * d + 8, :] = t
+
+
+def open_message(message, faces, place):
+    def one(b, carry):
+        for i in range(8):
+            faces[place + b, 1 + i // 4, i % 4] = unpack(
+                lambda d: message[b, 8 * d : 8 * d + 8, :], i, 8
+            )
+        for tile in range(4):
+            faces[place + b, 0, tile, 0:5, :] = message[b, 40 + 5 * tile : 45 + 5 * tile, :]
+        return carry
+
+    lax.fori_loop(0, 2, one, 0)
+
+
+def restrict(faces, down):
+    tiles = [t for b in range(2) for t in restrict_block(faces, b)]
+
+    def put(row, t):
+        down[row : row + t.shape[0], :] = t
+
+    store_message(tiles, put)
+
+
+def restrict_block(faces, b):
     row, lane = iotas()
     group, within, low = lane // 16, lane % 16, lane % 8
     second = (lane // 8) % 2
@@ -164,7 +256,7 @@
             t = t + pltpu.roll(t, 112, 1)
             halves.append(lanes_from(t, coarse + 2 * low))
         parts.append(jnp.where(group < 4, halves[0], halves[1]))
-    down[3 * b] = 0.25 * jnp.where(second == 0, parts[0], parts[1])
+    tiles = [0.25 * jnp.where(second == 0, parts[0], parts[1])]
     parts = []
     for side in range(2):
         rows = []
@@ -174,18 +266,23 @@
             t = t + pltpu.roll(t, 7, 0)
             rows.append(rows_from(lanes_from(t, fine), pair_rows))
         parts.append(jnp.where(row < 4, rows[0], rows[1]))
-    down[3 * b + 1] = 0.25 * jnp.where(second == 0, parts[0], parts[1])
+    tiles.append(0.25 * jnp.where(second == 0, parts[0], parts[1]))
     rows = []
     for a in range(2):
         halves = []
         for half in range(2):
             t = faces[2 + b, 2, a * 2 + half]
-            t = t + pltpu.roll(t, 112, 1)
-            halves.append(lanes_from(t, coarse + within))
-        t = jnp.where(group < 4, halves[0], halves[1])
+            t = t + pltpu.roll(t, 127, 1)
+            halves.append(lanes_from(t, group * 16 + second * 8 + 2 * (low % 4)))
+        t = jnp.where(low < 4, halves[0], halves[1])
         t = t + pltpu.roll(t, 7, 0)
         rows.append(rows_from(t, pair_rows))
-    down[3 * b + 2] = 0.25 * jnp.where(row < 4, rows[0], rows[1])
+    tiles.append(0.25 * jnp.where(row < 4, rows[0], rows[1]))
+    return tiles
+
+
+def member_offset(block, member):
+    return jnp.clip(lax.rem(lax.div(block, 2), NMEM) - member + 1, 0, 2)
 
 
 def slot_of(block, member):
@@ -194,17 +291,19 @@
     return jnp.clip(offset * 2 + lax.rem(safe, 2), 0, 5)
 
 
-def select_quadrants(faces, wanted, out, other, member):
+def select_quadrants(faces, wanted, out, other, asker, member, direct):
     row, lane = iotas()
     second = (lane // 8) % 2
+    tiles = []
     for b in range(2):
         for axis in range(3):
             parts = []
             for side in range(2):
-                code = jnp.maximum(wanted[other, b * 6 + 2 * axis + 1 - side], 0)
+                code = jnp.maximum(wanted[other, asker, b * 6 + 2 * axis + 1 - side], 0)
                 quadrant = lax.rem(code, 4)
                 first, last = lax.div(quadrant, 2), lax.rem(quadrant, 2)
-                slot = slot_of(lax.div(code, 4), member)
+                block = lax.div(code, 4)
+                slot = 2 + lax.rem(block, 2) if direct else slot_of(block, member)
                 if axis == 0:
                     tile = side * 2 + first
                 elif axis == 1:
@@ -215,10 +314,15 @@
                 if axis < 2:
                     t = pick(last == side, t, pltpu.roll(t, 8 if side else 120, 1))
                 parts.append(t)
-            out[other, b * 3 + axis] = jnp.where(second == 0, parts[0], parts[1])
-
-
-def build_halo(faces, up, down, halo, b, nbr, link, wanted, level, own, member):
+            tiles.append(jnp.where(second == 0, parts[0], parts[1]))
+
+    def put(row, t):
+        out[other, asker, row : row + t.shape[0], :] = t
+
+    store_message(tiles, put)
+
+
+def build_halo(faces, up, down, halo, b, nbr, link, wanted, level, own, member, direct):
     row, lane = iotas()
     group, within, low = lane // 16, lane % 16, lane % 8
     second = (lane // 8) % 2
@@ -226,35 +330,43 @@
 
     def link_state(j):
         code = wanted[b * 6 + j]
-        section = lax.div(lax.div(jnp.maximum(code, 0), 4), 2 * NMEM)
+        block = lax.div(jnp.maximum(code, 0), 4)
+        section = lax.div(block, 2 * NMEM)
+        offset = member_offset(block, member) if direct else 1
         any_link = code >= 0
         coarse = level[section] < own
-        return section, any_link, coarse
+        return section, offset, any_link, coarse
 
     def means(axis, j, k):
         block = link[b, k, j]
         safe = jnp.maximum(block, 0)
         section = lax.div(safe, 2 * NMEM)
-        offset = jnp.clip(lax.rem(lax.div(safe, 2), NMEM) - member + 1, 0, 2)
-        t = down[section, offset, lax.rem(safe, 2) * 3 + axis]
+        offset = member_offset(safe, member)
+        t = message_tile(
+            lambda row: down[section, offset, row : row + 8, :], axis, lax.rem(safe, 2)
+        )
         return pick(block >= 0, t, jnp.zeros_like(t))
 
     for axis in range(3):
         states, near, quads, ups = [], [], [], []
         for side in range(2):
             j = 2 * axis + 1 - side
-            section, any_link, coarse = link_state(j)
+            section, offset, any_link, coarse = link_state(j)
             states.append((nbr[b, j] >= 0, any_link, coarse))
             near.append(slot_of(nbr[b, j], member))
-            ups.append(up[section, b * 3 + axis])
+            ups.append(
+                message_tile(
+                    lambda row, section=section, offset=offset: up[section, offset, row : row + 8, :],
+                    axis,
+                    b,
+                )
+            )
             if down is not None:
                 quads.append([means(axis, j, k) for k in range(4)])
         if axis == 0:
             rest = jnp.where(row == 0, F32(1.0 / 18.0), F32(1.0 / 36.0))
-        elif axis == 1:
+        else:
             rest = jnp.where(group == 0, F32(1.0 / 18.0), F32(1.0 / 36.0))
-        else:
-            rest = jnp.where(low == 0, F32(1.0 / 18.0), F32(1.0 / 36.0))
 
         def choose(side, tile, from_up, from_down):
             is_near, any_link, coarse = states[side]
@@ -288,7 +400,7 @@
         else:
             both = jnp.where(second == 0, ups[0], ups[1])
             for half in range(2):
-                wide = lanes_from(both, (4 * half + group // 2) * 16 + within)
+                wide = lanes_from(both, group * 16 + second * 8 + 4 * half + low // 2)
                 for a in range(2):
                     tile = a * 2 + half
                     from_up = rows_from(wide, spread_rows[a])
@@ -311,15 +423,19 @@
             where = (row == (7 if far_end else 0)) & (group == p)
         elif one == 0:
             tiles = [(1 if far_end else 0) * 2 + half for half in range(2)]
-            where = (row == (7 if far_end else 0)) & (within == side * 8 + p)
+            where = (row == (7 if far_end else 0)) & (group == p) & (second == side)
         else:
             tiles = [a * 2 + (1 if far_end else 0) for a in range(2)]
-            where = lane == (7 if far_end else 0) * 16 + side * 8 + p
+            where = lane == p * 16 + side * 8 + (7 if far_end else 0)
         for tile in tiles:
             rows, lanes = tile_slices(two, tile)
             line = faces[slot, two, tile]
             line = pick(block >= 0, line, jnp.full_like(line, 1.0 / 36.0))
             halo[two, rows, lanes] = jnp.where(where, line, halo[two, rows, lanes])
+    order = face_order(lane)
+    for tile in range(4):
+        rows, lanes = tile_slices(2, tile)
+        halo[2, rows, lanes] = lanes_from(halo[2, rows, lanes], order)
 
 
 def stream(star, halo, out, b, advances, final):
@@ -400,6 +516,10 @@
     middle,
     faces_a,
     faces_b,
+    out_a,
+    out_b,
+    in_a,
+    in_b,
     up_send_a,
     up_send_b,
     up_a,
@@ -472,51 +592,51 @@
 
     def first_part(b, carry):
         collide(pop, mask_ref, star, b, rate, own >= 1, True)
-        export(star, faces_a, b)
-        restrict(faces_a, down_send, b)
+        export(star, faces_a, out_a, b)
         return carry
 
     lax.fori_loop(0, 2, first_part, 0)
+    restrict(faces_a, down_send)
 
     one = jnp.int32(1)
     there = jnp.where(m > 0, one, 0) + jnp.where(m < NMEM - 1, one, 0)
     pl.semaphore_wait(barrier, NSEC * (there + 1) - 1)
 
-    def meta_copy(place, other):
+    def meta_copy(place, offset, other, dm):
         return pltpu.make_async_remote_copy(
             src_ref=wanted_own,
-            dst_ref=wanted.at[place],
-            send_sem=meta_ss.at[other],
-            recv_sem=meta_rs.at[place],
-            device_id=(other, m),
+            dst_ref=wanted.at[place, offset],
+            send_sem=meta_ss.at[other, dm + 1],
+            recv_sem=meta_rs.at[place, offset],
+            device_id=(other, m + dm),
             device_id_type=MESH,
         )
 
-    def mem_copy(faces, step, dm, arriving):
-        into = (2 + 2 * dm) if arriving else (2 - 2 * dm)
+    def mem_copy(sends, receives, step, dm, arriving):
+        into = (1 + dm) // 2 if arriving else (1 - dm) // 2
         return pltpu.make_async_remote_copy(
-            src_ref=faces.at[pl.ds(2, 2)],
-            dst_ref=faces.at[pl.ds(into, 2)],
+            src_ref=sends,
+            dst_ref=receives.at[into],
             send_sem=mem_ss.at[step, (dm + 1) // 2],
-            recv_sem=mem_rs.at[step, into // 4],
+            recv_sem=mem_rs.at[step, into],
             device_id=(s, m + dm),
             device_id_type=MESH,
         )
 
-    def up_copy(sends, receives, step, other, place):
+    def up_copy(sends, receives, step, other, dm, place, offset):
         return pltpu.make_async_remote_copy(
-            src_ref=sends.at[other],
-            dst_ref=receives.at[place],
-            send_sem=up_ss.at[step, other],
-            recv_sem=up_rs.at[step, place],
-            device_id=(other, m),
+            src_ref=sends.at[other, dm + 1, pl.ds(0, 34)],
+            dst_ref=receives.at[place, offset, pl.ds(0, 34)],
+            send_sem=up_ss.at[step, other, dm + 1],
+            recv_sem=up_rs.at[step, place, offset],
+            device_id=(other, m + dm),
             device_id_type=MESH,
         )
 
     def down_copy(other, dm, place, offset):
         return pltpu.make_async_remote_copy(
-            src_ref=down_send,
-            dst_ref=down.at[place, offset],
+            src_ref=down_send.at[pl.ds(0, 34)],
+            dst_ref=down.at[place, offset, pl.ds(0, 34)],
             send_sem=down_ss.at[other, dm + 1],
             recv_sem=down_rs.at[place, offset],
             device_id=(other, m + dm),
@@ -530,9 +650,9 @@
 
         lax.fori_loop(low, high, step, 0)
 
-    each(0, s, lambda other: meta_copy(s, other).start())
+    each(0, s, lambda other: meta_copy(s, 1, other, 0).start())
     for dm in (-1, 1):
-        if_member(dm, lambda dm=dm: mem_copy(faces_a, 0, dm, False).start())
+        if_member(dm, lambda dm=dm: mem_copy(out_a, in_a, 0, dm, False).start())
 
     def start_down(other):
         for dm in (-1, 0, 1):
@@ -540,29 +660,43 @@
 
     each(1, s, start_down)
 
-    def exchange(faces, sends, receives, step, low, high):
+    def side_meta(do):
+        def both(other):
+            for dm in (-1, 1):
+                if_member(dm, lambda dm=dm: do(other, dm))
+
+        return both
+
+    each(1, s, side_meta(lambda other, dm: meta_copy(s, 1 - dm, other, dm).start()))
+
+    def receive_members(faces, receives, step):
         for dm in (-1, 1):
-            if_member(dm, lambda dm=dm: mem_copy(faces, step, dm, True).wait_recv())
-        if step == 0:
-            each(s + 1, NSEC, lambda other: meta_copy(other, s).wait_recv())
-
-        def send(other):
-            select_quadrants(faces, wanted, sends, other, m)
-            up_copy(sends, receives, step, other, s).start()
-
-        each(high, NSEC, send)
-        each(low, s, lambda other: up_copy(sends, receives, step, s, other).wait_recv())
-
-    exchange(faces_a, up_send_a, up_a, 0, 0, s + 1)
+
+            def take(dm=dm):
+                mem_copy(out_a, receives, step, dm, True).wait_recv()
+                open_message(receives.at[(1 + dm) // 2], faces, 2 + 2 * dm)
+
+            if_member(dm, take)
+
+    receive_members(faces_a, in_a, 0)
+    each(s + 1, NSEC, lambda other: meta_copy(other, 1, s, 0).wait_recv())
+
+    def send_up(other):
+        select_quadrants(faces_a, wanted, up_send_a, other, 1, m, False)
+        up_copy(up_send_a, up_a, 0, other, 0, s, 1).start()
+
+    each(s + 1, NSEC, send_up)
+    each(0, s, lambda other: up_copy(up_send_a, up_a, 0, s, 0, other, 1).wait_recv())
 
     def wait_down(other):
         for dm in (-1, 0, 1):
             if_member(dm, lambda dm=dm: down_copy(s, dm, other, dm + 1).wait_recv())
 
-    each(jnp.where(s == 0, NSEC, s + 1), NSEC, wait_down)
+    above = jnp.where(s == 0, NSEC, s + 1)
+    each(above, NSEC, wait_down)
 
     def second_part(b, carry):
-        build_halo(faces_a, up_a, down, halo, b, nbr, link, wanted_own, level, own, m)
+        build_halo(faces_a, up_a, down, halo, b, nbr, link, wanted_own, level, own, m, False)
         stream(star, halo, middle, b, own >= 1, False)
         return carry
 
@@ -570,43 +704,69 @@
 
     def third_part(b, carry):
         collide(middle, mask_ref, star, b, rate, own == 2, False)
-        export(star, faces_b, b)
+        export(star, faces_b, out_b, b)
         return carry
 
     lax.fori_loop(0, 2, third_part, 0)
     for dm in (-1, 1):
-        if_member(dm, lambda dm=dm: mem_copy(faces_b, 1, dm, False).start())
-    exchange(faces_b, up_send_b, up_b, 1, 1, jnp.where(s == 0, NSEC, s + 1))
+        if_member(dm, lambda dm=dm: mem_copy(out_b, in_b, 1, dm, False).start())
+    each(above, NSEC, side_meta(lambda other, dm: meta_copy(other, dm + 1, s, dm).wait_recv()))
+
+    def send_direct(other):
+        for dm in (-1, 0, 1):
+
+            def send(dm=dm):
+                select_quadrants(faces_b, wanted, up_send_b, other, dm + 1, m, True)
+                up_copy(up_send_b, up_b, 1, other, dm, s, 1 - dm).start()
+
+            if_member(dm, send)
+
+    each(above, NSEC, send_direct)
+    receive_members(faces_b, in_b, 1)
+
+    def wait_direct(other):
+        for dm in (-1, 0, 1):
+            if_member(
+                dm, lambda dm=dm: up_copy(up_send_b, up_b, 1, s, dm, other, dm + 1).wait_recv()
+            )
+
+    each(1, s, wait_direct)
 
     def fourth_part(b, carry):
-        build_halo(faces_b, up_b, None, halo, b, nbr, link, wanted_own, level, own, m)
+        build_halo(faces_b, up_b, None, halo, b, nbr, link, wanted_own, level, own, m, True)
         stream(star, halo, out, b, own == 2, True)
         return carry
 
     lax.fori_loop(0, 2, fourth_part, 0)
 
-    each(0, s, lambda other: meta_copy(s, other).wait_send())
+    each(0, s, lambda other: meta_copy(s, 1, other, 0).wait_send())
+    each(1, s, side_meta(lambda other, dm: meta_copy(s, 1 - dm, other, dm).wait_send()))
     for dm in (-1, 1):
-        if_member(dm, lambda dm=dm: mem_copy(faces_a, 0, dm, False).wait_send())
-        if_member(dm, lambda dm=dm: mem_copy(faces_b, 1, dm, False).wait_send())
+        if_member(dm, lambda dm=dm: mem_copy(out_a, in_a, 0, dm, False).wait_send())
+        if_member(dm, lambda dm=dm: mem_copy(out_b, in_b, 1, dm, False).wait_send())
 
     def end_down(other):
         for dm in (-1, 0, 1):
             if_member(dm, lambda dm=dm: down_copy(other, dm, s, 1 - dm).wait_send())
 
     each(1, s, end_down)
-    each(s + 1, NSEC, lambda other: up_copy(up_send_a, up_a, 0, other, s).wait_send())
-    each(
-        jnp.where(s == 0, NSEC, s + 1),
-        NSEC,
-        lambda other: up_copy(up_send_b, up_b, 1, other, s).wait_send(),
-    )
+    each(s + 1, NSEC, lambda other: up_copy(up_send_a, up_a, 0, other, 0, s, 1).wait_send())
+
+    def end_direct(other):
+        for dm in (-1, 0, 1):
+            if_member(
+                dm, lambda dm=dm: up_copy(up_send_b, up_b, 1, other, dm, s, 1 - dm).wait_send()
+            )
+
+    each(above, NSEC, end_direct)
 
 
 def body(populations, fluid_mask, section_level, neighbours, interface):
     state = pltpu.VMEM((2, 19, 16, 256), F32)
     faces = pltpu.VMEM((6, 3, 4, 8, 128), F32)
-    ups = pltpu.VMEM((NSEC, 6, 8, 128), F32)
+    ups = pltpu.VMEM((NSEC, 3, 40, 128), F32)
+    members = pltpu.VMEM((2, 60, 128), F32)
+    arrived = pltpu.VMEM((2, 2, 60, 128), F32)
     vmem = pl.BlockSpec(memory_space=pltpu.VMEM)
     hbm = pl.BlockSpec(memory_space=pltpu.HBM)
     dma = pltpu.SemaphoreType.DMA
@@ -626,21 +786,25 @@
             state,
             faces,
             faces,
+            members,
+            members,
+            arrived,
+            arrived,
             ups,
             ups,
             ups,
             ups,
-            pltpu.VMEM((6, 8, 128), F32),
-            pltpu.VMEM((NSEC, 3, 6, 8, 128), F32),
+            pltpu.VMEM((40, 128), F32),
+            ups,
             pltpu.VMEM((3, 16, 256), F32),
             pltpu.SMEM((12,), jnp.int32),
-            pltpu.SMEM((NSEC, 12), jnp.int32),
-            dma((NSEC,)),
-            dma((NSEC,)),
+            pltpu.SMEM((NSEC, 3, 12), jnp.int32),
+            dma((NSEC, 3)),
+            dma((NSEC, 3)),
             dma((2, 2)),
             dma((2, 2)),
-            dma((2, NSEC)),
-            dma((2, NSEC)),
+            dma((2, NSEC, 3)),
+            dma((2, NSEC, 3)),
             dma((NSEC, 3)),
             dma((NSEC, 3)),
         ],

time: 32.6 us -> 30.3 us (0.929); the launches traced: 32 us -> 30.1 us
  Pallas kernels: 30 us -> 28.2 us
    pallas_call x1, Pallas kernels: 30 us -> 28.2 us  [body(): pl.pallas_call(kernel, out_shape=jax.ShapeDtypeStruct((19, 64, 128), F32)...]
where the time goes in v2:
time: 30.3 us; the launch traced here: 30.1 us
  Pallas kernels  28.2 us (93%)
  local copies, waits for them, and re-layouts  1.96 us (6%)
    pallas_call x1, Pallas kernels, body(): pl.pallas_call(kernel, out_shape=jax.ShapeDtypeStruct((19, 64, 128), F32)...  28.2 us
    unnamed x1, local copies, waits for them, and re-layouts  1.96 us

profile of v2, /device:TPU:135, one launch (start us, length us, event | category | flops | bytes accessed | tf_op | source)
XLA Modules:
  0.0 30.1 jit_solution(5312177509902183421)
XLA Ops:
  0.0 28.2 %lattice_step.1 = f32[19,64,128]{2,1,0:T(8,128)} custom-call(f32[19,64,128]{2,1,0:T(8,128)} %bitcast.17, s32[64,128]{1,0:T(8,128)} %bitcast.18, s32[8]{0:T(128)} %level_hbm.1, s32[2,18]{1,0:T(2,128)} %nbr_hbm.1, s32[2,4,6]{2,1,0:T(4,128)} %bitcast.19), custom_call_target="tpu_custom_call" | custom-call | tf_op jit(solution)/shard_map/lattice_step/pallas_call | solution.py:773
  28.2 2.0 %copy.10 = f32[2,19,4096]{2,0,1:T(2,128)} copy(f32[2,19,4096]{2,0,1:T(2,128)} %bitcast.16) | data formatting | bytes 1245184

commit v3 on v2

--- a/solution.py
+++ b/solution.py
@@ -188,7 +188,7 @@
             for half in range(2):
                 line = star[b, q, layer : layer + 1, 128 * half : 128 * half + 128]
                 place = side * 2 + half
-                faces[2 + b, 0, place, p : p + 1, :] = line
+                faces[(2 + b) * 12 + place, p : p + 1, :] = line
                 message[b, 40 + 5 * place + p : 41 + 5 * place + p, :] = line
     zero = jnp.zeros((8, 128), F32)
     tiles = [None] * 8
@@ -213,7 +213,7 @@
                     total = jnp.where(within == side * 8 + p, x, total)
             tiles[4 + a * 2 + half] = lanes_from(total, order)
     for i, t in enumerate(tiles):
-        faces[2 + b, 1 + i // 4, i % 4] = t
+        faces[(2 + b) * 12 + 4 + i] = t
     for d, t in enumerate(pack(tiles)):
         message[b, 8 * d : 8 * d + 8, :] = t
 
@@ -221,11 +221,11 @@
 def open_message(message, faces, place):
     def one(b, carry):
         for i in range(8):
-            faces[place + b, 1 + i // 4, i % 4] = unpack(
+            faces[(place + b) * 12 + 4 + i] = unpack(
                 lambda d: message[b, 8 * d : 8 * d + 8, :], i, 8
             )
         for tile in range(4):
-            faces[place + b, 0, tile, 0:5, :] = message[b, 40 + 5 * tile : 45 + 5 * tile, :]
+            faces[(place + b) * 12 + tile, 0:5, :] = message[b, 40 + 5 * tile : 45 + 5 * tile, :]
         return carry
 
     lax.fori_loop(0, 2, one, 0)
@@ -251,7 +251,7 @@
     for side in range(2):
         halves = []
         for half in range(2):
-            t = faces[2 + b, 0, side * 2 + half]
+            t = faces[(2 + b) * 12 + side * 2 + half]
             t = t + pltpu.roll(t, 127, 1)
             t = t + pltpu.roll(t, 112, 1)
             halves.append(lanes_from(t, coarse + 2 * low))
@@ -261,7 +261,7 @@
     for side in range(2):
         rows = []
         for a in range(2):
-            t = faces[2 + b, 1, a * 2 + side]
+            t = faces[(2 + b) * 12 + 4 + a * 2 + side]
             t = t + pltpu.roll(t, 127, 1)
             t = t + pltpu.roll(t, 7, 0)
             rows.append(rows_from(lanes_from(t, fine), pair_rows))
@@ -271,7 +271,7 @@
     for a in range(2):
         halves = []
         for half in range(2):
-            t = faces[2 + b, 2, a * 2 + half]
+            t = faces[(2 + b) * 12 + 8 + a * 2 + half]
             t = t + pltpu.roll(t, 127, 1)
             halves.append(lanes_from(t, group * 16 + second * 8 + 2 * (low % 4)))
         t = jnp.where(low < 4, halves[0], halves[1])
@@ -282,37 +282,77 @@
 
 
 def member_offset(block, member):
-    return jnp.clip(lax.rem(lax.div(block, 2), NMEM) - member + 1, 0, 2)
+    return jnp.clip(((block >> 1) & (NMEM - 1)) - member + 1, 0, 2)
 
 
 def slot_of(block, member):
-    safe = jnp.maximum(block, 0)
-    offset = lax.rem(lax.div(safe, 2), NMEM) - member + 1
-    return jnp.clip(offset * 2 + lax.rem(safe, 2), 0, 5)
-
-
-def select_quadrants(faces, wanted, out, other, asker, member, direct):
-    row, lane = iotas()
+    return member_offset(block, member) * 2 + (block & 1)
+
+
+NEAR, STATE, UP_SAME, UP_DIRECT, DOWN, DOWN_BLOCK, EDGE, EDGE_THERE, TABLE = (
+    0,
+    6,
+    12,
+    18,
+    24,
+    48,
+    72,
+    84,
+    96,
+)
+
+
+def read_links(nbr, link, level, own, member, wanted, table, b):
+    section_shift = NMEM.bit_length()
+    for axis in range(3):
+        for side in range(2):
+            i, j = axis * 2 + side, axis * 2 + 1 - side
+            code = jnp.int32(-1)
+            for k in range(4):
+                block = link[b, k, j]
+                code = jnp.maximum(code, jnp.where(block >= 0, block * 4 + k, -1))
+                safe = jnp.maximum(block, 0)
+                place = (safe >> section_shift) * 3 + member_offset(safe, member)
+                table[b * TABLE + DOWN + i * 4 + k] = place
+                table[b * TABLE + DOWN_BLOCK + i * 4 + k] = jnp.where(block >= 0, safe & 1, -1)
+            safe = jnp.maximum(code, 0)
+            k, block = safe & 3, safe >> 2
+            section = block >> section_shift
+            first, last = k >> 1, k & 1
+            if axis == 0:
+                tile = side * 2 + first
+            elif axis == 1:
+                tile = 4 + first * 2 + side
+            else:
+                tile = 8 + k
+            wanted[b * 6 + i] = slot_of(block, member) * 12 + tile
+            wanted[12 + b * 6 + i] = (2 + (block & 1)) * 12 + tile
+            wanted[24 + b * 6 + i] = last
+            near = nbr[b, j]
+            table[b * TABLE + NEAR + i] = slot_of(jnp.maximum(near, 0), member) * 12
+            linked = jnp.where(code < 0, 3, jnp.where(level[section] < own, 1, 2))
+            table[b * TABLE + STATE + i] = jnp.where(near >= 0, 0, linked)
+            table[b * TABLE + UP_SAME + i] = section * 3 + 1
+            table[b * TABLE + UP_DIRECT + i] = section * 3 + member_offset(block, member)
+    for q in range(7, 19):
+        block = nbr[b, OPPOSITE[q] - 1]
+        table[b * TABLE + EDGE + q - 7] = slot_of(jnp.maximum(block, 0), member) * 12
+        table[b * TABLE + EDGE_THERE + q - 7] = block
+
+
+def select_quadrants(faces, wanted, out, other, asker, direct):
+    lane = iotas()[1]
     second = (lane // 8) % 2
     tiles = []
     for b in range(2):
         for axis in range(3):
             parts = []
             for side in range(2):
-                code = jnp.maximum(wanted[other, asker, b * 6 + 2 * axis + 1 - side], 0)
-                quadrant = lax.rem(code, 4)
-                first, last = lax.div(quadrant, 2), lax.rem(quadrant, 2)
-                block = lax.div(code, 4)
-                slot = 2 + lax.rem(block, 2) if direct else slot_of(block, member)
-                if axis == 0:
-                    tile = side * 2 + first
-                elif axis == 1:
-                    tile = first * 2 + side
-                else:
-                    tile = quadrant
-                t = faces[slot, axis, tile]
+                i = b * 6 + axis * 2 + side
+                t = faces[wanted[other, asker, (12 if direct else 0) + i]]
                 if axis < 2:
-                    t = pick(last == side, t, pltpu.roll(t, 8 if side else 120, 1))
+                    in_place = wanted[other, asker, 24 + i] == side
+                    t = pick(in_place, t, pltpu.roll(t, 8 if side else 120, 1))
                 parts.append(t)
             tiles.append(jnp.where(second == 0, parts[0], parts[1]))
 
@@ -322,57 +362,42 @@
     store_message(tiles, put)
 
 
-def build_halo(faces, up, down, halo, b, nbr, link, wanted, level, own, member, direct):
+def build_halo(faces, up, down, halo, b, table, direct):
     row, lane = iotas()
     group, within, low = lane // 16, lane % 16, lane % 8
     second = (lane // 8) % 2
     spread_rows = [4 * a + row // 2 for a in range(2)]
 
-    def link_state(j):
-        code = wanted[b * 6 + j]
-        block = lax.div(jnp.maximum(code, 0), 4)
-        section = lax.div(block, 2 * NMEM)
-        offset = member_offset(block, member) if direct else 1
-        any_link = code >= 0
-        coarse = level[section] < own
-        return section, offset, any_link, coarse
-
-    def means(axis, j, k):
-        block = link[b, k, j]
-        safe = jnp.maximum(block, 0)
-        section = lax.div(safe, 2 * NMEM)
-        offset = member_offset(safe, member)
-        t = message_tile(
-            lambda row: down[section, offset, row : row + 8, :], axis, lax.rem(safe, 2)
-        )
+    def entry(place):
+        return table[b * TABLE + place]
+
+    def means(axis, i, k):
+        place, block = entry(DOWN + i * 4 + k), entry(DOWN_BLOCK + i * 4 + k)
+        t = message_tile(lambda row: down[place, row : row + 8, :], axis, block)
         return pick(block >= 0, t, jnp.zeros_like(t))
 
     for axis in range(3):
         states, near, quads, ups = [], [], [], []
         for side in range(2):
-            j = 2 * axis + 1 - side
-            section, offset, any_link, coarse = link_state(j)
-            states.append((nbr[b, j] >= 0, any_link, coarse))
-            near.append(slot_of(nbr[b, j], member))
+            i = axis * 2 + side
+            states.append(entry(STATE + i))
+            near.append(entry(NEAR + i) + axis * 4)
+            place = entry((UP_DIRECT if direct else UP_SAME) + i)
             ups.append(
-                message_tile(
-                    lambda row, section=section, offset=offset: up[section, offset, row : row + 8, :],
-                    axis,
-                    b,
-                )
+                message_tile(lambda row, place=place: up[place, row : row + 8, :], axis, b)
             )
             if down is not None:
-                quads.append([means(axis, j, k) for k in range(4)])
+                quads.append([means(axis, i, k) for k in range(4)])
         if axis == 0:
             rest = jnp.where(row == 0, F32(1.0 / 18.0), F32(1.0 / 36.0))
         else:
             rest = jnp.where(group == 0, F32(1.0 / 18.0), F32(1.0 / 36.0))
 
         def choose(side, tile, from_up, from_down):
-            is_near, any_link, coarse = states[side]
-            linked = from_up if from_down is None else pick(coarse, from_up, from_down)
-            far = pick(any_link, linked, rest)
-            return pick(is_near, faces[near[side], axis, tile], far)
+            state = states[side]
+            far = rest if from_down is None else pick(state == 2, from_down, rest)
+            far = pick(state == 1, from_up, far)
+            return pick(state == 0, faces[near[side] + tile], far)
 
         if axis < 2:
             for side in range(2):
@@ -415,8 +440,7 @@
         c = VELOCITIES[q]
         one, two = [axis for axis in range(3) if c[axis]]
         side, p = side_of(q, two)
-        block = nbr[b, OPPOSITE[q] - 1]
-        slot = slot_of(block, member)
+        near, there = entry(EDGE + q - 7) + two * 4, entry(EDGE_THERE + q - 7) >= 0
         far_end = c[one] > 0
         if two == 1:
             tiles = [(1 if far_end else 0) * 2 + side]
@@ -429,8 +453,8 @@
             where = lane == p * 16 + side * 8 + (7 if far_end else 0)
         for tile in tiles:
             rows, lanes = tile_slices(two, tile)
-            line = faces[slot, two, tile]
-            line = pick(block >= 0, line, jnp.full_like(line, 1.0 / 36.0))
+            line = faces[near + tile]
+            line = pick(there, line, jnp.full_like(line, 1.0 / 36.0))
             halo[two, rows, lanes] = jnp.where(where, line, halo[two, rows, lanes])
     order = face_order(lane)
     for tile in range(4):
@@ -527,6 +551,7 @@
     down_send,
     down,
     halo,
+    table,
     wanted_own,
     wanted,
     meta_ss,
@@ -583,12 +608,6 @@
     rate = jnp.where(
         own == 0, F32(1.0 / 0.55), jnp.where(own == 1, F32(1.0 / 0.6), F32(1.0 / 0.7))
     )
-    for i in range(12):
-        code = jnp.int32(-1)
-        for k in range(4):
-            block = link[i // 6, k, i % 6]
-            code = jnp.maximum(code, jnp.where(block >= 0, block * 4 + k, -1))
-        wanted_own[i] = code
 
     def first_part(b, carry):
         collide(pop, mask_ref, star, b, rate, own >= 1, True)
@@ -597,6 +616,12 @@
 
     lax.fori_loop(0, 2, first_part, 0)
     restrict(faces_a, down_send)
+
+    def read(b, carry):
+        read_links(nbr, link, level, own, m, wanted_own, table, b)
+        return carry
+
+    lax.fori_loop(0, 2, read, 0)
 
     one = jnp.int32(1)
     there = jnp.where(m > 0, one, 0) + jnp.where(m < NMEM - 1, one, 0)
@@ -626,7 +651,7 @@
     def up_copy(sends, receives, step, other, dm, place, offset):
         return pltpu.make_async_remote_copy(
             src_ref=sends.at[other, dm + 1, pl.ds(0, 34)],
-            dst_ref=receives.at[place, offset, pl.ds(0, 34)],
+            dst_ref=receives.at[place * 3 + offset, pl.ds(0, 34)],
             send_sem=up_ss.at[step, other, dm + 1],
             recv_sem=up_rs.at[step, place, offset],
             device_id=(other, m + dm),
@@ -636,7 +661,7 @@
     def down_copy(other, dm, place, offset):
         return pltpu.make_async_remote_copy(
             src_ref=down_send.at[pl.ds(0, 34)],
-            dst_ref=down.at[place, offset, pl.ds(0, 34)],
+            dst_ref=down.at[place * 3 + offset, pl.ds(0, 34)],
             send_sem=down_ss.at[other, dm + 1],
             recv_sem=down_rs.at[place, offset],
             device_id=(other, m + dm),
@@ -682,7 +707,7 @@
     each(s + 1, NSEC, lambda other: meta_copy(other, 1, s, 0).wait_recv())
 
     def send_up(other):
-        select_quadrants(faces_a, wanted, up_send_a, other, 1, m, False)
+        select_quadrants(faces_a, wanted, up_send_a, other, 1, False)
         up_copy(up_send_a, up_a, 0, other, 0, s, 1).start()
 
     each(s + 1, NSEC, send_up)
@@ -696,7 +721,7 @@
     each(above, NSEC, wait_down)
 
     def second_part(b, carry):
-        build_halo(faces_a, up_a, down, halo, b, nbr, link, wanted_own, level, own, m, False)
+        build_halo(faces_a, up_a, down, halo, b, table, False)
         stream(star, halo, middle, b, own >= 1, False)
         return carry
 
@@ -716,7 +741,7 @@
         for dm in (-1, 0, 1):
 
             def send(dm=dm):
-                select_quadrants(faces_b, wanted, up_send_b, other, dm + 1, m, True)
+                select_quadrants(faces_b, wanted, up_send_b, other, dm + 1, True)
                 up_copy(up_send_b, up_b, 1, other, dm, s, 1 - dm).start()
 
             if_member(dm, send)
@@ -730,15 +755,6 @@
                 dm, lambda dm=dm: up_copy(up_send_b, up_b, 1, s, dm, other, dm + 1).wait_recv()
             )
 
-    each(1, s, wait_direct)
-
-    def fourth_part(b, carry):
-        build_halo(faces_b, up_b, None, halo, b, nbr, link, wanted_own, level, own, m, True)
-        stream(star, halo, out, b, own == 2, True)
-        return carry
-
-    lax.fori_loop(0, 2, fourth_part, 0)
-
     each(0, s, lambda other: meta_copy(s, 1, other, 0).wait_send())
     each(1, s, side_meta(lambda other, dm: meta_copy(s, 1 - dm, other, dm).wait_send()))
     for dm in (-1, 1):
@@ -759,12 +775,21 @@
             )
 
     each(above, NSEC, end_direct)
+    each(1, s, wait_direct)
+
+    def fourth_part(b, carry):
+        build_halo(faces_b, up_b, None, halo, b, table, True)
+        stream(star, halo, out, b, own == 2, True)
+        return carry
+
+    lax.fori_loop(0, 2, fourth_part, 0)
 
 
 def body(populations, fluid_mask, section_level, neighbours, interface):
     state = pltpu.VMEM((2, 19, 16, 256), F32)
-    faces = pltpu.VMEM((6, 3, 4, 8, 128), F32)
+    faces = pltpu.VMEM((72, 8, 128), F32)
     ups = pltpu.VMEM((NSEC, 3, 40, 128), F32)
+    came = pltpu.VMEM((NSEC * 3, 40, 128), F32)
     members = pltpu.VMEM((2, 60, 128), F32)
     arrived = pltpu.VMEM((2, 2, 60, 128), F32)
     vmem = pl.BlockSpec(memory_space=pltpu.VMEM)
@@ -792,13 +817,14 @@
             arrived,
             ups,
             ups,
-            ups,
-            ups,
+            came,
+            came,
             pltpu.VMEM((40, 128), F32),
-            ups,
+            came,
             pltpu.VMEM((3, 16, 256), F32),
-            pltpu.SMEM((12,), jnp.int32),
-            pltpu.SMEM((NSEC, 3, 12), jnp.int32),
+            pltpu.SMEM((2 * TABLE,), jnp.int32),
+            pltpu.SMEM((36,), jnp.int32),
+            pltpu.SMEM((NSEC, 3, 36), jnp.int32),
             dma((NSEC, 3)),
             dma((NSEC, 3)),
             dma((2, 2)),

time: 30.3 us -> 29.3 us (0.967)
  Pallas kernels: 28.2 us -> 27.2 us
    pallas_call x1, Pallas kernels: 28.2 us -> 27.2 us  [body(): pl.pallas_call(kernel, out_shape=jax.ShapeDtypeStruct((19, 64, 128), F32)...]
where the time goes in v3:
time: 29.3 us; the launch traced here: 29.1 us
  Pallas kernels  27.2 us (93%)
  local copies, waits for them, and re-layouts  1.96 us (7%)
    pallas_call x1, Pallas kernels, body(): pl.pallas_call(kernel, out_shape=jax.ShapeDtypeStruct((19, 64, 128), F32)...  27.2 us
    unnamed x1, local copies, waits for them, and re-layouts  1.96 us

profile of v3, /device:TPU:135, one launch (start us, length us, event | category | flops | bytes accessed | tf_op | source)
XLA Modules:
  0.0 29.1 jit_solution(10256436103082736580)
XLA Ops:
  0.0 27.2 %lattice_step.1 = f32[19,64,128]{2,1,0:T(8,128)} custom-call(f32[19,64,128]{2,1,0:T(8,128)} %bitcast.17, s32[64,128]{1,0:T(8,128)} %bitcast.18, s32[8]{0:T(128)} %level_hbm.1, s32[2,18]{1,0:T(2,128)} %nbr_hbm.1, s32[2,4,6]{2,1,0:T(4,128)} %bitcast.19), custom_call_target="tpu_custom_call" | custom-call | tf_op jit(solution)/shard_map/lattice_step/pallas_call | solution.py:798
  27.2 2.0 %copy.10 = f32[2,19,4096]{2,0,1:T(2,128)} copy(f32[2,19,4096]{2,0,1:T(2,128)} %bitcast.16) | data formatting | bytes 1245184

commit v4 on v3

--- a/solution.py
+++ b/solution.py
@@ -302,8 +302,10 @@
 )
 
 
-def read_links(nbr, link, level, own, member, wanted, table, b):
-    section_shift = NMEM.bit_length()
+SECTION_SHIFT = NMEM.bit_length()
+
+
+def read_wanted(link, member, wanted, table, b):
     for axis in range(3):
         for side in range(2):
             i, j = axis * 2 + side, axis * 2 + 1 - side
@@ -311,13 +313,9 @@
             for k in range(4):
                 block = link[b, k, j]
                 code = jnp.maximum(code, jnp.where(block >= 0, block * 4 + k, -1))
-                safe = jnp.maximum(block, 0)
-                place = (safe >> section_shift) * 3 + member_offset(safe, member)
-                table[b * TABLE + DOWN + i * 4 + k] = place
-                table[b * TABLE + DOWN_BLOCK + i * 4 + k] = jnp.where(block >= 0, safe & 1, -1)
+            table[b * TABLE + STATE + i] = code
             safe = jnp.maximum(code, 0)
             k, block = safe & 3, safe >> 2
-            section = block >> section_shift
             first, last = k >> 1, k & 1
             if axis == 0:
                 tile = side * 2 + first
@@ -328,11 +326,26 @@
             wanted[b * 6 + i] = slot_of(block, member) * 12 + tile
             wanted[12 + b * 6 + i] = (2 + (block & 1)) * 12 + tile
             wanted[24 + b * 6 + i] = last
+
+
+def read_links(nbr, link, level, own, member, table, b):
+    for axis in range(3):
+        for side in range(2):
+            i, j = axis * 2 + side, axis * 2 + 1 - side
+            for k in range(4):
+                block = link[b, k, j]
+                safe = jnp.maximum(block, 0)
+                place = (safe >> SECTION_SHIFT) * 3 + member_offset(safe, member)
+                table[b * TABLE + DOWN + i * 4 + k] = place
+                table[b * TABLE + DOWN_BLOCK + i * 4 + k] = jnp.where(block >= 0, safe & 1, -1)
+            code = table[b * TABLE + STATE + i]
+            block = jnp.maximum(code, 0) >> 2
+            section = block >> SECTION_SHIFT
             near = nbr[b, j]
             table[b * TABLE + NEAR + i] = slot_of(jnp.maximum(near, 0), member) * 12
             linked = jnp.where(code < 0, 3, jnp.where(level[section] < own, 1, 2))
             table[b * TABLE + STATE + i] = jnp.where(near >= 0, 0, linked)
-            table[b * TABLE + UP_SAME + i] = section * 3 + 1
+            table[b * TABLE + UP_SAME + i] = section
             table[b * TABLE + UP_DIRECT + i] = section * 3 + member_offset(block, member)
     for q in range(7, 19):
         block = nbr[b, OPPOSITE[q] - 1]
@@ -340,7 +353,7 @@
         table[b * TABLE + EDGE_THERE + q - 7] = block
 
 
-def select_quadrants(faces, wanted, out, other, asker, direct):
+def select_quadrants(faces, ask, out, place, direct):
     lane = iotas()[1]
     second = (lane // 8) % 2
     tiles = []
@@ -349,15 +362,14 @@
             parts = []
             for side in range(2):
                 i = b * 6 + axis * 2 + side
-                t = faces[wanted[other, asker, (12 if direct else 0) + i]]
+                t = faces[ask((12 if direct else 0) + i)]
                 if axis < 2:
-                    in_place = wanted[other, asker, 24 + i] == side
-                    t = pick(in_place, t, pltpu.roll(t, 8 if side else 120, 1))
+                    t = pick(ask(24 + i) == side, t, pltpu.roll(t, 8 if side else 120, 1))
                 parts.append(t)
             tiles.append(jnp.where(second == 0, parts[0], parts[1]))
 
     def put(row, t):
-        out[other, asker, row : row + t.shape[0], :] = t
+        out[place, row : row + t.shape[0], :] = t
 
     store_message(tiles, put)
 
@@ -554,12 +566,17 @@
     table,
     wanted_own,
     wanted,
+    wanted_side,
+    mem_ss,
+    mem_rs,
+    side_ss,
+    side_rs,
     meta_ss,
     meta_rs,
-    mem_ss,
-    mem_rs,
-    up_ss,
-    up_rs,
+    up_a_ss,
+    up_a_rs,
+    up_b_ss,
+    up_b_rs,
     down_ss,
     down_rs,
 ):
@@ -569,8 +586,8 @@
         pltpu.make_async_copy(src, dst, in_sems.at[i])
         for i, (src, dst) in enumerate(
             [
+                (link_hbm, link),
                 (level_hbm, level),
-                (link_hbm, link),
                 (nbr_hbm, nbr),
                 (pop_hbm, pop),
                 (mask_hbm, mask_ref),
@@ -580,6 +597,8 @@
     for load in loads:
         load.start()
     has = {-1: m > 0, 0: None, 1: m < NMEM - 1}
+    one = jnp.int32(1)
+    around = 1 + jnp.where(has[-1], one, 0) + jnp.where(has[1], one, 0)
 
     def if_member(dm, do):
         if has[dm] is None:
@@ -587,112 +606,108 @@
         else:
             pl.when(has[dm])(do)
 
+    def each(low, high, do):
+        def step(i, carry):
+            do(i)
+            return carry
+
+        lax.fori_loop(low, high, step, 0)
+
+    def blocks(do):
+        each(0, 2, do)
+
     barrier = pltpu.get_barrier_semaphore()
 
-    def greet(other, dm):
-        pl.semaphore_signal(barrier, inc=1, device_id=(other, m + dm), device_id_type=MESH)
-
-    def greet_section(other, carry):
-        @pl.when(other != s)
-        def _():
-            greet(other, 0)
-
+    def greet(other):
+        def signal(dm):
+            pl.semaphore_signal(barrier, inc=1, device_id=(other, m + dm), device_id_type=MESH)
+
+        pl.when(other != s)(lambda: signal(0))
         for dm in (-1, 1):
-            if_member(dm, lambda dm=dm: greet(other, dm))
-        return carry
-
-    lax.fori_loop(0, NSEC, greet_section, 0)
-    for load in loads:
+            if_member(dm, lambda dm=dm: signal(dm))
+
+    each(0, NSEC, greet)
+
+    def remote(src, dst, send_sem, recv_sem, other, dm):
+        return pltpu.make_async_remote_copy(
+            src_ref=src,
+            dst_ref=dst,
+            send_sem=send_sem,
+            recv_sem=recv_sem,
+            device_id=(other, m + dm),
+            device_id_type=MESH,
+        )
+
+    def message(ref, place):
+        return ref.at[place, pl.ds(0, 34)]
+
+    def meta_copy(src, dst, other):
+        return remote(src, dst, meta_ss, meta_rs, other, 0)
+
+    def side_copy(dm, arriving):
+        into = (1 + dm) // 2 if arriving else (1 - dm) // 2
+        return remote(
+            wanted, wanted_side.at[into], side_ss.at[(dm + 1) // 2], side_rs.at[into], s, dm
+        )
+
+    def mem_copy(sends, receives, step, dm, arriving):
+        into = (1 + dm) // 2 if arriving else (1 - dm) // 2
+        return remote(
+            sends,
+            receives.at[into],
+            mem_ss.at[step, (dm + 1) // 2],
+            mem_rs.at[step, into],
+            s,
+            dm,
+        )
+
+    def up_a_copy(src, dst, other):
+        return remote(src, dst, up_a_ss, up_a_rs, other, 0)
+
+    def up_b_copy(src, dst, other, dm):
+        return remote(src, dst, up_b_ss, up_b_rs, other, dm)
+
+    def down_copy(src, dst, other, dm):
+        return remote(src, dst, down_ss, down_rs, other, dm)
+
+    singles = tuple(range(1, NSEC))
+    groups = tuple(sorted({k * e for k in range(1, NSEC - 1) for e in (2, 3)}))
+
+    def wait_group(count, cases, ref, copy, receive):
+        for n in cases:
+
+            @pl.when(count == n)
+            def _(n=n):
+                whole = ref.at[pl.ds(0, n), pl.ds(0, 34)] if len(ref.shape) == 3 else ref.at[pl.ds(0, n)]
+                both = copy(whole, whole)
+                both.wait_recv() if receive else both.wait_send()
+
+    below = s
+    higher = NSEC - 1 - s
+    below_direct = jnp.maximum(s - 1, 0)
+    above = jnp.where(s == 0, NSEC, s + 1)
+    higher_direct = NSEC - above
+
+    for load in loads[:3]:
         load.wait()
     own = level[s]
     rate = jnp.where(
         own == 0, F32(1.0 / 0.55), jnp.where(own == 1, F32(1.0 / 0.6), F32(1.0 / 0.7))
     )
-
-    def first_part(b, carry):
+    blocks(lambda b: read_wanted(link, m, wanted_own, table, b))
+    for load in loads[3:]:
+        load.wait()
+
+    def first_part(b):
         collide(pop, mask_ref, star, b, rate, own >= 1, True)
         export(star, faces_a, out_a, b)
-        return carry
-
-    lax.fori_loop(0, 2, first_part, 0)
-    restrict(faces_a, down_send)
-
-    def read(b, carry):
-        read_links(nbr, link, level, own, m, wanted_own, table, b)
-        return carry
-
-    lax.fori_loop(0, 2, read, 0)
-
-    one = jnp.int32(1)
-    there = jnp.where(m > 0, one, 0) + jnp.where(m < NMEM - 1, one, 0)
-    pl.semaphore_wait(barrier, NSEC * (there + 1) - 1)
-
-    def meta_copy(place, offset, other, dm):
-        return pltpu.make_async_remote_copy(
-            src_ref=wanted_own,
-            dst_ref=wanted.at[place, offset],
-            send_sem=meta_ss.at[other, dm + 1],
-            recv_sem=meta_rs.at[place, offset],
-            device_id=(other, m + dm),
-            device_id_type=MESH,
-        )
-
-    def mem_copy(sends, receives, step, dm, arriving):
-        into = (1 + dm) // 2 if arriving else (1 - dm) // 2
-        return pltpu.make_async_remote_copy(
-            src_ref=sends,
-            dst_ref=receives.at[into],
-            send_sem=mem_ss.at[step, (dm + 1) // 2],
-            recv_sem=mem_rs.at[step, into],
-            device_id=(s, m + dm),
-            device_id_type=MESH,
-        )
-
-    def up_copy(sends, receives, step, other, dm, place, offset):
-        return pltpu.make_async_remote_copy(
-            src_ref=sends.at[other, dm + 1, pl.ds(0, 34)],
-            dst_ref=receives.at[place * 3 + offset, pl.ds(0, 34)],
-            send_sem=up_ss.at[step, other, dm + 1],
-            recv_sem=up_rs.at[step, place, offset],
-            device_id=(other, m + dm),
-            device_id_type=MESH,
-        )
-
-    def down_copy(other, dm, place, offset):
-        return pltpu.make_async_remote_copy(
-            src_ref=down_send.at[pl.ds(0, 34)],
-            dst_ref=down.at[place * 3 + offset, pl.ds(0, 34)],
-            send_sem=down_ss.at[other, dm + 1],
-            recv_sem=down_rs.at[place, offset],
-            device_id=(other, m + dm),
-            device_id_type=MESH,
-        )
-
-    def each(low, high, do):
-        def step(i, carry):
-            do(i)
-            return carry
-
-        lax.fori_loop(low, high, step, 0)
-
-    each(0, s, lambda other: meta_copy(s, 1, other, 0).start())
-    for dm in (-1, 1):
-        if_member(dm, lambda dm=dm: mem_copy(out_a, in_a, 0, dm, False).start())
-
-    def start_down(other):
-        for dm in (-1, 0, 1):
-            if_member(dm, lambda dm=dm: down_copy(other, dm, s, 1 - dm).start())
-
-    each(1, s, start_down)
-
-    def side_meta(do):
-        def both(other):
-            for dm in (-1, 1):
-                if_member(dm, lambda dm=dm: do(other, dm))
-
-        return both
-
-    each(1, s, side_meta(lambda other, dm: meta_copy(s, 1 - dm, other, dm).start()))
+
+    blocks(first_part)
+    pl.semaphore_wait(barrier, NSEC * around - 1)
+
+    def start_members(sends, receives, step):
+        for dm in (-1, 1):
+            if_member(dm, lambda dm=dm: mem_copy(sends, receives, step, dm, False).start())
 
     def receive_members(faces, receives, step):
         for dm in (-1, 1):
@@ -703,93 +718,101 @@
 
             if_member(dm, take)
 
+    each(0, s, lambda other: meta_copy(wanted_own, wanted.at[s], other).start())
+    start_members(out_a, in_a, 0)
+    restrict(faces_a, down_send)
+
+    def start_down(other):
+        for dm in (-1, 0, 1):
+            if_member(
+                dm,
+                lambda dm=dm: down_copy(
+                    down_send.at[pl.ds(0, 34)], message(down, s * 3 + 1 - dm), other, dm
+                ).start(),
+            )
+
+    each(1, s, start_down)
+    blocks(lambda b: read_links(nbr, link, level, own, m, table, b))
     receive_members(faces_a, in_a, 0)
-    each(s + 1, NSEC, lambda other: meta_copy(other, 1, s, 0).wait_recv())
+    wait_group(higher, singles, wanted, lambda x, y: meta_copy(x, y, s), True)
 
     def send_up(other):
-        select_quadrants(faces_a, wanted, up_send_a, other, 1, False)
-        up_copy(up_send_a, up_a, 0, other, 0, s, 1).start()
+        select_quadrants(faces_a, lambda i: wanted[other, i], up_send_a, other, False)
+        up_a_copy(message(up_send_a, other), message(up_a, s), other).start()
 
     each(s + 1, NSEC, send_up)
-    each(0, s, lambda other: up_copy(up_send_a, up_a, 0, s, 0, other, 1).wait_recv())
-
-    def wait_down(other):
-        for dm in (-1, 0, 1):
-            if_member(dm, lambda dm=dm: down_copy(s, dm, other, dm + 1).wait_recv())
-
-    above = jnp.where(s == 0, NSEC, s + 1)
-    each(above, NSEC, wait_down)
-
-    def second_part(b, carry):
+    for dm in (-1, 1):
+        if_member(dm, lambda dm=dm: side_copy(dm, False).start())
+    wait_group(below, singles, up_a, lambda x, y: up_a_copy(x, y, s), True)
+    wait_group(
+        jnp.where(s == 0, 0, higher) * around,
+        groups,
+        down,
+        lambda x, y: down_copy(x, y, s, 0),
+        True,
+    )
+
+    def second_part(b):
         build_halo(faces_a, up_a, down, halo, b, table, False)
         stream(star, halo, middle, b, own >= 1, False)
-        return carry
-
-    lax.fori_loop(0, 2, second_part, 0)
-
-    def third_part(b, carry):
+
+    blocks(second_part)
+
+    def third_part(b):
         collide(middle, mask_ref, star, b, rate, own == 2, False)
         export(star, faces_b, out_b, b)
-        return carry
-
-    lax.fori_loop(0, 2, third_part, 0)
+
+    blocks(third_part)
+    start_members(out_b, in_b, 1)
     for dm in (-1, 1):
-        if_member(dm, lambda dm=dm: mem_copy(out_b, in_b, 1, dm, False).start())
-    each(above, NSEC, side_meta(lambda other, dm: meta_copy(other, dm + 1, s, dm).wait_recv()))
+        if_member(dm, lambda dm=dm: side_copy(dm, True).wait_recv())
 
     def send_direct(other):
         for dm in (-1, 0, 1):
 
             def send(dm=dm):
-                select_quadrants(faces_b, wanted, up_send_b, other, dm + 1, True)
-                up_copy(up_send_b, up_b, 1, other, dm, s, 1 - dm).start()
+                def ask(i):
+                    return wanted[other, i] if dm == 0 else wanted_side[(1 + dm) // 2, other, i]
+
+                place = other * 3 + dm + 1
+                select_quadrants(faces_b, ask, up_send_b, place, True)
+                up_b_copy(
+                    message(up_send_b, place), message(up_b, s * 3 + 1 - dm), other, dm
+                ).start()
 
             if_member(dm, send)
 
     each(above, NSEC, send_direct)
-    receive_members(faces_b, in_b, 1)
-
-    def wait_direct(other):
-        for dm in (-1, 0, 1):
-            if_member(
-                dm, lambda dm=dm: up_copy(up_send_b, up_b, 1, s, dm, other, dm + 1).wait_recv()
-            )
-
-    each(0, s, lambda other: meta_copy(s, 1, other, 0).wait_send())
-    each(1, s, side_meta(lambda other, dm: meta_copy(s, 1 - dm, other, dm).wait_send()))
+    wait_group(below, singles, wanted, lambda x, y: meta_copy(x, y, s), False)
     for dm in (-1, 1):
         if_member(dm, lambda dm=dm: mem_copy(out_a, in_a, 0, dm, False).wait_send())
+        if_member(dm, lambda dm=dm: side_copy(dm, False).wait_send())
+    wait_group(
+        below_direct * around, groups, down, lambda x, y: down_copy(x, y, s, 0), False
+    )
+    wait_group(higher, singles, up_send_a, lambda x, y: up_a_copy(x, y, s), False)
+    receive_members(faces_b, in_b, 1)
+    for dm in (-1, 1):
         if_member(dm, lambda dm=dm: mem_copy(out_b, in_b, 1, dm, False).wait_send())
-
-    def end_down(other):
-        for dm in (-1, 0, 1):
-            if_member(dm, lambda dm=dm: down_copy(other, dm, s, 1 - dm).wait_send())
-
-    each(1, s, end_down)
-    each(s + 1, NSEC, lambda other: up_copy(up_send_a, up_a, 0, other, 0, s, 1).wait_send())
-
-    def end_direct(other):
-        for dm in (-1, 0, 1):
-            if_member(
-                dm, lambda dm=dm: up_copy(up_send_b, up_b, 1, other, dm, s, 1 - dm).wait_send()
-            )
-
-    each(above, NSEC, end_direct)
-    each(1, s, wait_direct)
-
-    def fourth_part(b, carry):
+    wait_group(
+        higher_direct * around, groups, up_send_b, lambda x, y: up_b_copy(x, y, s, 0), False
+    )
+    wait_group(
+        below_direct * around, groups, up_b, lambda x, y: up_b_copy(x, y, s, 0), True
+    )
+
+    def fourth_part(b):
         build_halo(faces_b, up_b, None, halo, b, table, True)
         stream(star, halo, out, b, own == 2, True)
-        return carry
-
-    lax.fori_loop(0, 2, fourth_part, 0)
+
+    blocks(fourth_part)
 
 
 def body(populations, fluid_mask, section_level, neighbours, interface):
     state = pltpu.VMEM((2, 19, 16, 256), F32)
     faces = pltpu.VMEM((72, 8, 128), F32)
-    ups = pltpu.VMEM((NSEC, 3, 40, 128), F32)
-    came = pltpu.VMEM((NSEC * 3, 40, 128), F32)
+    by_section = pltpu.VMEM((NSEC, 40, 128), F32)
+    by_device = pltpu.VMEM((NSEC * 3, 40, 128), F32)
     members = pltpu.VMEM((2, 60, 128), F32)
     arrived = pltpu.VMEM((2, 2, 60, 128), F32)
     vmem = pl.BlockSpec(memory_space=pltpu.VMEM)
@@ -815,27 +838,25 @@
             members,
             arrived,
             arrived,
-            ups,
-            ups,
-            came,
-            came,
+            by_section,
+            by_device,
+            by_section,
+            by_device,
             pltpu.VMEM((40, 128), F32),
-            came,
+            by_device,
             pltpu.VMEM((3, 16, 256), F32),
             pltpu.SMEM((2 * TABLE,), jnp.int32),
-            pltpu.SMEM((36,), jnp.int32),
-            pltpu.SMEM((NSEC, 3, 36), jnp.int32),
-            dma((NSEC, 3)),
-            dma((NSEC, 3)),
+            pltpu.SMEM((128,), jnp.int32),
+            pltpu.SMEM((NSEC, 128), jnp.int32),
+            pltpu.SMEM((2, NSEC, 128), jnp.int32),
             dma((2, 2)),
             dma((2, 2)),
-            dma((2, NSEC, 3)),
-            dma((2, NSEC, 3)),
-            dma((NSEC, 3)),
-            dma((NSEC, 3)),
-        ],
+            dma((2,)),
+            dma((2,)),
+        ]
+        + [dma] * 8,
         compiler_params=pltpu.CompilerParams(
-            collective_id=0, has_side_effects=True, vmem_limit_bytes=62 * 1024 * 1024
+            collective_id=0, has_side_effects=True, vmem_limit_bytes=54400 * 1024
         ),
         name="lattice_step",
     )(

time: 29.3 us -> 27 us (0.922)
  Pallas kernels: 27.2 us -> 24.5 us
  local copies, waits for them, and re-layouts: 1.96 us -> 2.28 us
    pallas_call x1, Pallas kernels: 27.2 us -> 24.5 us  [body(): pl.pallas_call(kernel, out_shape=jax.ShapeDtypeStruct((19, 64, 128), F32)...]
    unnamed x1 -> x9, local copies, waits for them, and re-layouts: 1.96 us -> 2.28 us
where the time goes in v4:
time: 27 us; the launch traced here: 26.8 us
  Pallas kernels  24.5 us (91%)
  local copies, waits for them, and re-layouts  2.28 us (8%)
    pallas_call x1, Pallas kernels, body(): pl.pallas_call(kernel, out_shape=jax.ShapeDtypeStruct((19, 64, 128), F32)...  24.5 us
    unnamed x9, local copies, waits for them, and re-layouts  2.28 us

profile of v4, /device:TPU:135, one launch (start us, length us, event | category | flops | bytes accessed | tf_op | source)
XLA Modules:
  0.0 26.8 jit_solution(1638417592332290416)
XLA Ops:
  0.0 0.0 copy-start.1
  0.0 0.0 copy-start.2
  0.0 0.0 copy-start.3
  0.0 0.7 %copy-done.1 = s32[2,6,4]{1,2,0:T(4,128)S(1)} copy-done((s32[2,6,4]{1,2,0:T(4,128)S(1)}, s32[2,6,4]{1,2,0:T(4,128)}, u32[]{:S(2)}) %copy-start.1) | copy-done | bytes 216
  0.7 0.0 copy-done.2
  0.7 0.0 copy-done.3
  0.7 0.0 copy-start
  0.7 0.8 %copy-done = s32[2,4096]{1,0:T(2,128)S(1)} copy-done((s32[2,4096]{1,0:T(2,128)S(1)}, s32[2,4096]{1,0:T(2,128)}, u32[]{:S(2)}) %copy-start) | copy-done | bytes 32792
  1.5 24.5 %lattice_step.1 = f32[19,64,128]{2,1,0:T(8,128)S(1)} custom-call(f32[19,64,128]{2,1,0:T(8,128)} %bitcast.19, s32[64,128]{1,0:T(8,128)S(1)} %bitcast.17, s32[8]{0:T(128)S(1)} %copy-done.3, s32[2,18]{1,0:T(2,128)S(1)} %copy-done.2, s32[2,4,6]{2,1,0:T(4,128)S(1)} %bitcast.18), custom_call_target="tpu_custom_call" | custom-call | tf_op jit(solution)/shard_map/lattice_step/pallas_call | solution.py:821
  26.0 0.8 %copy.10 = f32[2,19,4096]{2,0,1:T(2,128)} copy(f32[2,19,4096]{2,0,1:T(2,128)S(1)} %bitcast.16) | data formatting | bytes 1245184
Async XLA Ops:
  0.0 0.7 %copy-start.1 = (s32[2,6,4]{1,2,0:T(4,128)S(1)}, s32[2,6,4]{1,2,0:T(4,128)}, u32[]{:S(2)}) copy-start(s32[2,6,4]{1,2,0:T(4,128)} %param.9) | copy-start | bytes 580
  0.0 0.7 %copy-start.2 = (s32[2,18]{1,0:T(2,128)S(1)}, s32[2,18]{1,0:T(2,128)}, u32[]{:S(2)}) copy-start(s32[2,18]{1,0:T(2,128)} %nbr_hbm.1) | copy-start | bytes 436
  0.0 0.7 %copy-start.3 = (s32[8]{0:T(128)S(1)}, s32[8]{0:T(128)}, u32[]{:S(2)}) copy-start(s32[8]{0:T(128)} %level_hbm.1) | copy-start | bytes 100
  0.7 0.8 %copy-start = (s32[2,4096]{1,0:T(2,128)S(1)}, s32[2,4096]{1,0:T(2,128)}, u32[]{:S(2)}) copy-start(s32[2,4096]{1,0:T(2,128)} %param.6) | copy-start | bytes 98308

commit v5 on v4

--- a/solution.py
+++ b/solution.py
@@ -820,7 +820,7 @@
     dma = pltpu.SemaphoreType.DMA
     out = pl.pallas_call(
         kernel,
-        out_shape=jax.ShapeDtypeStruct((19, 64, 128), F32),
+        out_shape=pltpu.VMEM((19, 64, 128), F32),
         in_specs=[hbm] * 5,
         out_specs=vmem,
         scratch_shapes=[
@@ -856,7 +856,7 @@
         ]
         + [dma] * 8,
         compiler_params=pltpu.CompilerParams(
-            collective_id=0, has_side_effects=True, vmem_limit_bytes=54400 * 1024
+            collective_id=0, has_side_effects=True, vmem_limit_bytes=54656 * 1024
         ),
         name="lattice_step",
     )(

time: 27 us -> 25.4 us (0.941)
  local copies, waits for them, and re-layouts: 2.28 us -> 0.83 us
    unnamed x9 -> x1, local copies, waits for them, and re-layouts: 2.28 us -> 0.83 us
where the time goes in v5:
time: 25.4 us; the launch traced here: 25.3 us
  Pallas kernels  24.4 us (96%)
  local copies, waits for them, and re-layouts  0.83 us (3%)
    pallas_call x1, Pallas kernels, body(): pl.pallas_call(kernel, out_shape=pltpu.VMEM((19, 64, 128), F32), in_specs...  24.4 us
    unnamed x1, local copies, waits for them, and re-layouts  0.83 us

profile of v5, /device:TPU:135, one launch (start us, length us, event | category | flops | bytes accessed | tf_op | source)
XLA Modules:
  0.0 25.3 jit_solution(3730698872279730747)
XLA Ops:
  0.0 24.4 %lattice_step.1 = f32[19,64,128]{2,1,0:T(8,128)S(1)} custom-call(f32[19,64,128]{2,1,0:T(8,128)} %bitcast.17, s32[64,128]{1,0:T(8,128)} %bitcast.18, s32[8]{0:T(128)} %level_hbm.1, s32[2,18]{1,0:T(2,128)} %nbr_hbm.1, s32[2,4,6]{2,1,0:T(4,128)} %bitcast.19), custom_call_target="tpu_custom_call" | custom-call | tf_op jit(solution)/shard_map/lattice_step/pallas_call | solution.py:821
  24.4 0.8 %copy.10 = f32[2,19,4096]{2,0,1:T(2,128)} copy(f32[2,19,4096]{2,0,1:T(2,128)S(1)} %bitcast.16) | data formatting | bytes 1245184

commit v6 on v5

--- a/solution.py
+++ b/solution.py
@@ -374,11 +374,60 @@
     store_message(tiles, put)
 
 
-def build_halo(faces, up, down, halo, b, table, direct):
+def edge_place(q):
+    row, lane = iotas()
+    group, second = lane // 16, (lane // 8) % 2
+    c = VELOCITIES[q]
+    one, two = [axis for axis in range(3) if c[axis]]
+    side, p = side_of(q, two)
+    end, line = (1, 7) if c[one] > 0 else (0, 0)
+    if two == 1:
+        return two, [(end * 2 + side, (row == line) & (group == p))]
+    if one == 0:
+        cells = (row == line) & (group == p) & (second == side)
+        return two, [(end * 2 + half, cells) for half in range(2)]
+    return two, [(a * 2 + end, lane == p * 16 + side * 8 + line) for a in range(2)]
+
+
+def build_near(faces, halo, b, table):
+    row, lane = iotas()
+    group, second = lane // 16, (lane // 8) % 2
+
+    def entry(place):
+        return table[b * TABLE + place]
+
+    for axis in range(3):
+        rest = jnp.where((row if axis == 0 else group) == 0, F32(1.0 / 18.0), F32(1.0 / 36.0))
+        for tile in range(4):
+            sides = [tile // 2] if axis == 0 else [tile % 2] if axis == 1 else [0, 1]
+            parts = []
+            for side in sides:
+                i = axis * 2 + side
+                t = faces[entry(NEAR + i) + axis * 4 + tile]
+                parts.append(pick(entry(STATE + i) == 0, t, rest))
+            t = parts[0] if axis < 2 else jnp.where(second == 0, parts[0], parts[1])
+            rows, lanes = tile_slices(axis, tile)
+            halo[b, axis, rows, lanes] = t
+    for q in range(7, 19):
+        two, places = edge_place(q)
+        near, there = entry(EDGE + q - 7) + two * 4, entry(EDGE_THERE + q - 7) >= 0
+        for tile, cells in places:
+            rows, lanes = tile_slices(two, tile)
+            line = faces[near + tile]
+            line = pick(there, line, jnp.full_like(line, 1.0 / 36.0))
+            halo[b, two, rows, lanes] = jnp.where(cells, line, halo[b, two, rows, lanes])
+
+
+def build_links(up, down, halo, b, table, direct):
     row, lane = iotas()
     group, within, low = lane // 16, lane % 16, lane % 8
     second = (lane // 8) % 2
     spread_rows = [4 * a + row // 2 for a in range(2)]
+    edges = {}
+    for q in range(7, 19):
+        two, places = edge_place(q)
+        for tile, cells in places:
+            edges[two, tile] = edges[two, tile] | cells if (two, tile) in edges else cells
 
     def entry(place):
         return table[b * TABLE + place]
@@ -389,27 +438,33 @@
         return pick(block >= 0, t, jnp.zeros_like(t))
 
     for axis in range(3):
-        states, near, quads, ups = [], [], [], []
+        states, quads, ups = [], [], []
         for side in range(2):
             i = axis * 2 + side
             states.append(entry(STATE + i))
-            near.append(entry(NEAR + i) + axis * 4)
             place = entry((UP_DIRECT if direct else UP_SAME) + i)
             ups.append(
                 message_tile(lambda row, place=place: up[place, row : row + 8, :], axis, b)
             )
             if down is not None:
                 quads.append([means(axis, i, k) for k in range(4)])
-        if axis == 0:
-            rest = jnp.where(row == 0, F32(1.0 / 18.0), F32(1.0 / 36.0))
-        else:
-            rest = jnp.where(group == 0, F32(1.0 / 18.0), F32(1.0 / 36.0))
-
-        def choose(side, tile, from_up, from_down):
+
+        def choose(side, old, from_up, from_down):
             state = states[side]
-            far = rest if from_down is None else pick(state == 2, from_down, rest)
-            far = pick(state == 1, from_up, far)
-            return pick(state == 0, faces[near[side] + tile], far)
+            t = old if from_down is None else pick(state == 2, from_down, old)
+            return pick(state == 1, from_up, t)
+
+        def put(tile, old, t):
+            if (axis, tile) in edges:
+                t = jnp.where(edges[axis, tile], old, t)
+            if axis == 2:
+                t = lanes_from(t, face_order(lane))
+            rows, lanes = tile_slices(axis, tile)
+            halo[b, axis, rows, lanes] = t
+
+        def present(tile):
+            rows, lanes = tile_slices(axis, tile)
+            return halo[b, axis, rows, lanes]
 
         if axis < 2:
             for side in range(2):
@@ -432,8 +487,8 @@
                         else:
                             high_part = pltpu.roll(high_part, 8, 1)
                         from_down = jnp.where(second == 0, low_part, high_part)
-                    rows, lanes = tile_slices(axis, tile)
-                    halo[axis, rows, lanes] = choose(side, tile, from_up, from_down)
+                    old = present(tile)
+                    put(tile, old, choose(side, old, from_up, from_down))
         else:
             both = jnp.where(second == 0, ups[0], ups[1])
             for half in range(2):
@@ -441,98 +496,86 @@
                 for a in range(2):
                     tile = a * 2 + half
                     from_up = rows_from(wide, spread_rows[a])
+                    old = present(tile)
                     parts = [
-                        choose(side, tile, from_up, quads[side][tile] if down is not None else None)
+                        choose(side, old, from_up, quads[side][tile] if down is not None else None)
                         for side in range(2)
                     ]
-                    rows, lanes = tile_slices(axis, tile)
-                    halo[axis, rows, lanes] = jnp.where(second == 0, parts[0], parts[1])
-
-    for q in range(7, 19):
+                    put(tile, old, jnp.where(second == 0, parts[0], parts[1]))
+
+
+def roll(x, shift, axis):
+    shift %= x.shape[axis]
+    return pltpu.roll(x, shift, axis) if shift else x
+
+
+def ring(left, right, sign):
+    lane = iotas(left.shape)[1]
+    a, c = roll(left, 16 * sign, 1), roll(right, 16 * sign, 1)
+    if sign > 0:
+        return [jnp.where(lane < 16, c, a), jnp.where(lane < 16, a, c)]
+    return [jnp.where(lane >= 112, c, a), jnp.where(lane >= 112, a, c)]
+
+
+def drift(star, moved, b, advances):
+    for q in range(1, 19):
         c = VELOCITIES[q]
-        one, two = [axis for axis in range(3) if c[axis]]
-        side, p = side_of(q, two)
-        near, there = entry(EDGE + q - 7) + two * 4, entry(EDGE_THERE + q - 7) >= 0
-        far_end = c[one] > 0
-        if two == 1:
-            tiles = [(1 if far_end else 0) * 2 + side]
-            where = (row == (7 if far_end else 0)) & (group == p)
-        elif one == 0:
-            tiles = [(1 if far_end else 0) * 2 + half for half in range(2)]
-            where = (row == (7 if far_end else 0)) & (group == p) & (second == side)
-        else:
-            tiles = [a * 2 + (1 if far_end else 0) for a in range(2)]
-            where = lane == p * 16 + side * 8 + (7 if far_end else 0)
-        for tile in tiles:
-            rows, lanes = tile_slices(two, tile)
-            line = faces[near + tile]
-            line = pick(there, line, jnp.full_like(line, 1.0 / 36.0))
-            halo[two, rows, lanes] = jnp.where(where, line, halo[two, rows, lanes])
-    order = face_order(lane)
-    for tile in range(4):
-        rows, lanes = tile_slices(2, tile)
-        halo[2, rows, lanes] = lanes_from(halo[2, rows, lanes], order)
-
-
-def stream(star, halo, out, b, advances, final):
+        old = [star[b, q, :, 128 * half : 128 * half + 128] for half in range(2)]
+        new = [roll(t, c[0], 0) for t in old]
+        if c[1]:
+            new = ring(new[0], new[1], c[1])
+        for half in range(2):
+            t = roll(new[half], c[2], 1)
+            moved[b, q, :, 128 * half : 128 * half + 128] = pick(advances, t, old[half])
+    moved[b, 0] = star[b, 0]
+
+
+def finish(moved, halo, out, b, advances, final):
     row, lane = iotas((16, 128))
-    within = lane % 16
+    row = pick(advances, row, jnp.full_like(row, -1))
+    within = pick(advances, lane % 16, jnp.full_like(lane, 8))
+    lane = pick(advances, lane, jnp.full_like(lane, 64))
     first, last = lane < 16, lane >= 112
-
-    def roll(x, shift, axis):
-        shift %= x.shape[axis]
-        return pltpu.roll(x, shift, axis) if shift else x
-
-    def ring(left, right, sign):
-        a, c = roll(left, 16 * sign, 1), roll(right, 16 * sign, 1)
-        if sign > 0:
-            return jnp.where(first, c, a), jnp.where(first, a, c)
-        return jnp.where(last, c, a), jnp.where(last, a, c)
 
     for q in range(19):
         c = VELOCITIES[q]
-        old = [star[b, q, :, 128 * half : 128 * half + 128] for half in range(2)]
-        new = list(old)
+        new = [moved[b, q, :, 128 * half : 128 * half + 128] for half in range(2)]
         if c[0]:
             side, p = side_of(q, 0)
             place = side * 8 + p
+            plane = [
+                halo[b, 0, place : place + 1, 128 * half : 128 * half + 128] for half in range(2)
+            ]
+            if c[1]:
+                plane = ring(plane[0], plane[1], c[1])
             for half in range(2):
-                plane = halo[0, place : place + 1, 128 * half : 128 * half + 128]
-                moved = roll(new[half], c[0], 0)
-                new[half] = jnp.where(row == (0 if c[0] > 0 else 15), plane, moved)
+                line = roll(plane[half], c[2], 1)
+                new[half] = jnp.where(row == (0 if c[0] > 0 else 15), line, new[half])
         if c[1]:
             side, p = side_of(q, 1)
-            border = halo[1, :, 128 * side : 128 * side + 128]
-            border = roll(border, -16 * p if side == 0 else 112 - 16 * p, 1)
-            if c[0]:
-                border = roll(border, c[0], 0)
-            a, d = roll(new[0], 16 * c[1], 1), roll(new[1], 16 * c[1], 1)
-            if c[1] > 0:
-                new = [jnp.where(first, border, a), jnp.where(first, a, d)]
-            else:
-                new = [jnp.where(last, d, a), jnp.where(last, border, d)]
+            border = halo[b, 1, :, 128 * side : 128 * side + 128]
+            border = roll(border, (-16 * p if side == 0 else 112 - 16 * p) + c[2], 1)
+            border = roll(border, c[0], 0)
+            new[side] = jnp.where(last if side else first, border, new[side])
         if c[2]:
             side, p = side_of(q, 2)
             borders = []
             for half in range(2):
-                border = halo[2, :, 128 * half : 128 * half + 128]
+                border = halo[b, 2, :, 128 * half : 128 * half + 128]
                 border = roll(border, -p if side == 0 else 7 - p, 1)
-                if c[0]:
-                    border = roll(border, c[0], 0)
-                borders.append(border)
+                borders.append(roll(border, c[0], 0))
             if c[1]:
                 borders = ring(borders[0], borders[1], c[1])
             for half in range(2):
                 new[half] = jnp.where(
-                    within == (0 if c[2] > 0 else 15), borders[half], roll(new[half], c[2], 1)
+                    within == (0 if c[2] > 0 else 15), borders[half], new[half]
                 )
         for half in range(2):
-            result = pick(advances, new[half], old[half])
             if final:
                 for a in range(2):
-                    out[q, woven(b, 2 * a + half), :] = result[8 * a : 8 * a + 8]
-            else:
-                out[b, q, :, 128 * half : 128 * half + 128] = result
+                    out[q, woven(b, 2 * a + half), :] = new[half][8 * a : 8 * a + 8]
+            elif q:
+                out[b, q, :, 128 * half : 128 * half + 128] = new[half]
 
 
 def kernel(
@@ -743,6 +786,11 @@
     each(s + 1, NSEC, send_up)
     for dm in (-1, 1):
         if_member(dm, lambda dm=dm: side_copy(dm, False).start())
+    def prepare_first(b):
+        drift(star, middle, b, own >= 1)
+        build_near(faces_a, halo, b, table)
+
+    blocks(prepare_first)
     wait_group(below, singles, up_a, lambda x, y: up_a_copy(x, y, s), True)
     wait_group(
         jnp.where(s == 0, 0, higher) * around,
@@ -753,8 +801,8 @@
     )
 
     def second_part(b):
-        build_halo(faces_a, up_a, down, halo, b, table, False)
-        stream(star, halo, middle, b, own >= 1, False)
+        build_links(up_a, down, halo, b, table, False)
+        finish(middle, halo, middle, b, own >= 1, False)
 
     blocks(second_part)
 
@@ -783,6 +831,7 @@
             if_member(dm, send)
 
     each(above, NSEC, send_direct)
+    blocks(lambda b: drift(star, middle, b, own == 2))
     wait_group(below, singles, wanted, lambda x, y: meta_copy(x, y, s), False)
     for dm in (-1, 1):
         if_member(dm, lambda dm=dm: mem_copy(out_a, in_a, 0, dm, False).wait_send())
@@ -792,6 +841,7 @@
     )
     wait_group(higher, singles, up_send_a, lambda x, y: up_a_copy(x, y, s), False)
     receive_members(faces_b, in_b, 1)
+    blocks(lambda b: build_near(faces_b, halo, b, table))
     for dm in (-1, 1):
         if_member(dm, lambda dm=dm: mem_copy(out_b, in_b, 1, dm, False).wait_send())
     wait_group(
@@ -802,8 +852,8 @@
     )
 
     def fourth_part(b):
-        build_halo(faces_b, up_b, None, halo, b, table, True)
-        stream(star, halo, out, b, own == 2, True)
+        build_links(up_b, None, halo, b, table, True)
+        finish(middle, halo, out, b, own == 2, True)
 
     blocks(fourth_part)
 
@@ -844,7 +894,7 @@
             by_device,
             pltpu.VMEM((40, 128), F32),
             by_device,
-            pltpu.VMEM((3, 16, 256), F32),
+            pltpu.VMEM((2, 3, 16, 256), F32),
             pltpu.SMEM((2 * TABLE,), jnp.int32),
             pltpu.SMEM((128,), jnp.int32),
             pltpu.SMEM((NSEC, 128), jnp.int32),

time: 25.4 us -> 25.4 us (level)
  no operation moved by 1% of the time
where the time goes in v6:
time: 25.4 us; the launch traced here: 25.3 us
  Pallas kernels  24.4 us (96%)
  local copies, waits for them, and re-layouts  0.83 us (3%)
    pallas_call x1, Pallas kernels, body(): pl.pallas_call(kernel, out_shape=pltpu.VMEM((19, 64, 128), F32), in_specs...  24.4 us
    unnamed x1, local copies, waits for them, and re-layouts  0.83 us

profile of v6, /device:TPU:135, one launch (start us, length us, event | category | flops | bytes accessed | tf_op | source)
XLA Modules:
  0.0 25.3 jit_solution(13062108376824624552)
XLA Ops:
  0.0 24.4 %lattice_step.1 = f32[19,64,128]{2,1,0:T(8,128)S(1)} custom-call(f32[19,64,128]{2,1,0:T(8,128)} %bitcast.17, s32[64,128]{1,0:T(8,128)} %bitcast.18, s32[8]{0:T(128)} %level_hbm.1, s32[2,18]{1,0:T(2,128)} %nbr_hbm.1, s32[2,4,6]{2,1,0:T(4,128)} %bitcast.19), custom_call_target="tpu_custom_call" | custom-call | tf_op jit(solution)/shard_map/lattice_step/pallas_call | solution.py:871
  24.4 0.8 %copy.10 = f32[2,19,4096]{2,0,1:T(2,128)} copy(f32[2,19,4096]{2,0,1:T(2,128)S(1)} %bitcast.16) | data formatting | bytes 1245184

commit v7 on v6

--- a/solution.py
+++ b/solution.py
@@ -116,11 +116,10 @@
 
 
 def message_tile(load, axis, block):
-    if axis == 0:
-        pair = load(24), load(29)
-    else:
-        pair = tuple(unpack(lambda d: load(8 * d), 2 * b + axis - 1, 4) for b in range(2))
-    return pick(block == 0, pair[0], pair[1])
+    def tile(b):
+        return load(24 + 5 * b) if axis == 0 else unpack(lambda d: load(8 * d), 2 * b + axis - 1, 4)
+
+    return tile(block) if isinstance(block, int) else pick(block == 0, tile(0), tile(1))
 
 
 def face_order(lane):
@@ -219,16 +218,13 @@
 
 
 def open_message(message, faces, place):
-    def one(b, carry):
+    for b in range(2):
         for i in range(8):
             faces[(place + b) * 12 + 4 + i] = unpack(
                 lambda d: message[b, 8 * d : 8 * d + 8, :], i, 8
             )
         for tile in range(4):
             faces[(place + b) * 12 + tile, 0:5, :] = message[b, 40 + 5 * tile : 45 + 5 * tile, :]
-        return carry
-
-    lax.fori_loop(0, 2, one, 0)
 
 
 def restrict(faces, down):
@@ -657,7 +653,8 @@
         lax.fori_loop(low, high, step, 0)
 
     def blocks(do):
-        each(0, 2, do)
+        for b in range(2):
+            do(b)
 
     barrier = pltpu.get_barrier_semaphore()
 

time: 25.4 us -> 24.4 us (0.961)
  Pallas kernels: 24.4 us -> 23.4 us
    pallas_call x1, Pallas kernels: 24.4 us -> 23.4 us  [body(): pl.pallas_call(kernel, out_shape=pltpu.VMEM((19, 64, 128), F32), in_specs...]
where the time goes in v7:
time: 24.4 us; the launch traced here: 24.3 us
  Pallas kernels  23.4 us (96%)
  local copies, waits for them, and re-layouts  0.83 us (3%)
    pallas_call x1, Pallas kernels, body(): pl.pallas_call(kernel, out_shape=pltpu.VMEM((19, 64, 128), F32), in_specs...  23.4 us
    unnamed x1, local copies, waits for them, and re-layouts  0.83 us

profile of v7, /device:TPU:135, one launch (start us, length us, event | category | flops | bytes accessed | tf_op | source)
XLA Modules:
  0.0 24.3 jit_solution(6004924293405986772)
XLA Ops:
  0.0 23.4 %lattice_step.1 = f32[19,64,128]{2,1,0:T(8,128)S(1)} custom-call(f32[19,64,128]{2,1,0:T(8,128)} %bitcast.17, s32[64,128]{1,0:T(8,128)} %bitcast.18, s32[8]{0:T(128)} %level_hbm.1, s32[2,18]{1,0:T(2,128)} %nbr_hbm.1, s32[2,4,6]{2,1,0:T(4,128)} %bitcast.19), custom_call_target="tpu_custom_call" | custom-call | tf_op jit(solution)/shard_map/lattice_step/pallas_call | solution.py:868
  23.4 0.8 %copy.10 = f32[2,19,4096]{2,0,1:T(2,128)} copy(f32[2,19,4096]{2,0,1:T(2,128)S(1)} %bitcast.16) | data formatting | bytes 1245184

commit v8 on v7

--- a/solution.py
+++ b/solution.py
@@ -751,12 +751,9 @@
 
     def receive_members(faces, receives, step):
         for dm in (-1, 1):
-
-            def take(dm=dm):
-                mem_copy(out_a, receives, step, dm, True).wait_recv()
-                open_message(receives.at[(1 + dm) // 2], faces, 2 + 2 * dm)
-
-            if_member(dm, take)
+            if_member(dm, lambda dm=dm: mem_copy(out_a, receives, step, dm, True).wait_recv())
+        for dm in (-1, 1):
+            open_message(receives.at[(1 + dm) // 2], faces, 2 + 2 * dm)
 
     each(0, s, lambda other: meta_copy(wanted_own, wanted.at[s], other).start())
     start_members(out_a, in_a, 0)
@@ -797,17 +794,10 @@
         True,
     )
 
-    def second_part(b):
-        build_links(up_a, down, halo, b, table, False)
-        finish(middle, halo, middle, b, own >= 1, False)
-
-    blocks(second_part)
-
-    def third_part(b):
-        collide(middle, mask_ref, star, b, rate, own == 2, False)
-        export(star, faces_b, out_b, b)
-
-    blocks(third_part)
+    blocks(lambda b: build_links(up_a, down, halo, b, table, False))
+    blocks(lambda b: finish(middle, halo, middle, b, own >= 1, False))
+    blocks(lambda b: collide(middle, mask_ref, star, b, rate, own == 2, False))
+    blocks(lambda b: export(star, faces_b, out_b, b))
     start_members(out_b, in_b, 1)
     for dm in (-1, 1):
         if_member(dm, lambda dm=dm: side_copy(dm, True).wait_recv())
@@ -848,11 +838,8 @@
         below_direct * around, groups, up_b, lambda x, y: up_b_copy(x, y, s, 0), True
     )
 
-    def fourth_part(b):
-        build_links(up_b, None, halo, b, table, True)
-        finish(middle, halo, out, b, own == 2, True)
-
-    blocks(fourth_part)
+    blocks(lambda b: build_links(up_b, None, halo, b, table, True))
+    blocks(lambda b: finish(middle, halo, out, b, own == 2, True))
 
 
 def body(populations, fluid_mask, section_level, neighbours, interface):

time: 24.4 us -> 24.2 us (level)
  no operation moved by 1% of the time
where the time goes in v8:
time: 24.2 us; the launch traced here: 24.1 us
  Pallas kernels  23.3 us (96%)
  local copies, waits for them, and re-layouts  0.83 us (3%)
    pallas_call x1, Pallas kernels, body(): pl.pallas_call(kernel, out_shape=pltpu.VMEM((19, 64, 128), F32), in_specs...  23.3 us
    unnamed x1, local copies, waits for them, and re-layouts  0.83 us

profile of v8, /device:TPU:135, one launch (start us, length us, event | category | flops | bytes accessed | tf_op | source)
XLA Modules:
  0.0 24.1 jit_solution(16505058061754439710)
XLA Ops:
  0.0 23.3 %lattice_step.1 = f32[19,64,128]{2,1,0:T(8,128)S(1)} custom-call(f32[19,64,128]{2,1,0:T(8,128)} %bitcast.17, s32[64,128]{1,0:T(8,128)} %bitcast.18, s32[8]{0:T(128)} %level_hbm.1, s32[2,18]{1,0:T(2,128)} %nbr_hbm.1, s32[2,4,6]{2,1,0:T(4,128)} %bitcast.19), custom_call_target="tpu_custom_call" | custom-call | tf_op jit(solution)/shard_map/lattice_step/pallas_call | solution.py:855
  23.3 0.8 %copy.10 = f32[2,19,4096]{2,0,1:T(2,128)} copy(f32[2,19,4096]{2,0,1:T(2,128)S(1)} %bitcast.16) | data formatting | bytes 1245184

commit v9 on v8

--- a/solution.py
+++ b/solution.py
@@ -805,14 +805,20 @@
     def send_direct(other):
         for dm in (-1, 0, 1):
 
+            def ask(i, dm=dm):
+                if dm == 0:
+                    return wanted[other, i]
+                return jnp.where(has[dm], wanted_side[(1 + dm) // 2, other, i], 0)
+
+            select_quadrants(faces_b, ask, up_send_b, other * 3 + dm + 1, True)
+        for dm in (-1, 0, 1):
+
             def send(dm=dm):
-                def ask(i):
-                    return wanted[other, i] if dm == 0 else wanted_side[(1 + dm) // 2, other, i]
-
-                place = other * 3 + dm + 1
-                select_quadrants(faces_b, ask, up_send_b, place, True)
                 up_b_copy(
-                    message(up_send_b, place), message(up_b, s * 3 + 1 - dm), other, dm
+                    message(up_send_b, other * 3 + dm + 1),
+                    message(up_b, s * 3 + 1 - dm),
+                    other,
+                    dm,
                 ).start()
 
             if_member(dm, send)

time: 24.2 us -> 24 us (level)
  no operation moved by 1% of the time
where the time goes in v9:
time: 24 us; the launch traced here: 23.9 us
  Pallas kernels  23.1 us (96%)
  local copies, waits for them, and re-layouts  0.83 us (3%)
    pallas_call x1, Pallas kernels, body(): pl.pallas_call(kernel, out_shape=pltpu.VMEM((19, 64, 128), F32), in_specs...  23.1 us
    unnamed x1, local copies, waits for them, and re-layouts  0.83 us

profile of v9, /device:TPU:135, one launch (start us, length us, event | category | flops | bytes accessed | tf_op | source)
XLA Modules:
  0.0 23.9 jit_solution(7007096710487535373)
XLA Ops:
  0.0 23.1 %lattice_step.1 = f32[19,64,128]{2,1,0:T(8,128)S(1)} custom-call(f32[19,64,128]{2,1,0:T(8,128)} %bitcast.17, s32[64,128]{1,0:T(8,128)} %bitcast.18, s32[8]{0:T(128)} %level_hbm.1, s32[2,18]{1,0:T(2,128)} %nbr_hbm.1, s32[2,4,6]{2,1,0:T(4,128)} %bitcast.19), custom_call_target="tpu_custom_call" | custom-call | tf_op jit(solution)/shard_map/lattice_step/pallas_call | solution.py:861
  23.1 0.8 %copy.10 = f32[2,19,4096]{2,0,1:T(2,128)} copy(f32[2,19,4096]{2,0,1:T(2,128)S(1)} %bitcast.16) | data formatting | bytes 1245184

commit v10 on v9

--- a/solution.py
+++ b/solution.py
@@ -773,11 +773,18 @@
     receive_members(faces_a, in_a, 0)
     wait_group(higher, singles, wanted, lambda x, y: meta_copy(x, y, s), True)
 
-    def send_up(other):
+    def send_up(pair):
+        other = s + 1 + 2 * pair
+        later = jnp.minimum(other + 1, NSEC - 1)
         select_quadrants(faces_a, lambda i: wanted[other, i], up_send_a, other, False)
+        select_quadrants(faces_a, lambda i: wanted[later, i], up_send_a, other + 1, False)
         up_a_copy(message(up_send_a, other), message(up_a, s), other).start()
 
-    each(s + 1, NSEC, send_up)
+        @pl.when(other + 1 < NSEC)
+        def _():
+            up_a_copy(message(up_send_a, other + 1), message(up_a, s), other + 1).start()
+
+    each(0, (NSEC - s) // 2, send_up)
     for dm in (-1, 1):
         if_member(dm, lambda dm=dm: side_copy(dm, False).start())
     def prepare_first(b):
@@ -878,7 +885,7 @@
             members,
             arrived,
             arrived,
-            by_section,
+            pltpu.VMEM((NSEC + 1, 40, 128), F32),
             by_device,
             by_section,
             by_device,

time: 24 us -> 24 us (level)
  no operation moved by 1% of the time
where the time goes in v10:
time: 24 us; the launch traced here: 23.9 us
  Pallas kernels  23.1 us (96%)
  local copies, waits for them, and re-layouts  0.83 us (3%)
    pallas_call x1, Pallas kernels, body(): pl.pallas_call(kernel, out_shape=pltpu.VMEM((19, 64, 128), F32), in_specs...  23.1 us
    unnamed x1, local copies, waits for them, and re-layouts  0.83 us

profile of v10, /device:TPU:135, one launch (start us, length us, event | category | flops | bytes accessed | tf_op | source)
XLA Modules:
  0.0 23.9 jit_solution(17408476755800519550)
XLA Ops:
  0.0 23.1 %lattice_step.1 = f32[19,64,128]{2,1,0:T(8,128)S(1)} custom-call(f32[19,64,128]{2,1,0:T(8,128)} %bitcast.17, s32[64,128]{1,0:T(8,128)} %bitcast.18, s32[8]{0:T(128)} %level_hbm.1, s32[2,18]{1,0:T(2,128)} %nbr_hbm.1, s32[2,4,6]{2,1,0:T(4,128)} %bitcast.19), custom_call_target="tpu_custom_call" | custom-call | tf_op jit(solution)/shard_map/lattice_step/pallas_call | solution.py:868
  23.1 0.8 %copy.10 = f32[2,19,4096]{2,0,1:T(2,128)} copy(f32[2,19,4096]{2,0,1:T(2,128)S(1)} %bitcast.16) | data formatting | bytes 1245184
